TPU v7x, 32 devices: a whole 2x2x4 slice. The times are simulated.
32 devices in a mesh: row: 8 (over z, x), col: 4 (over y, core).
Axes of the slice: x: 2, y: 2, z: 4, core: 2. Of those that a mesh axis runs over, the one named last changes fastest.
Arguments:
- measured: bfloat16 [128, 32, 16, 512], P('col', 'row'), may hold values from 0 to 2
- module_row: int32 [32], replicated, may hold values from 0 to 31, each once
- scan_offsets: int32 [8, 4, 4, 2], P('row', 'col'), may hold values from 0 to 511, as said below
- specimen: float32 [2, 2048, 2048], P(None, 'row', 'col'), may hold values from -9.3 to 9.3
- illumination: float32 [2, 512, 512], replicated, may hold values from -4 to 4
Outputs:
- specimen_step: float32 [2, 2048, 2048], P(None, 'row', 'col')
- illumination_step: float32 [2, 512, 512], replicated
Inputs may be any that keep to these rules, and one draw needn't show every extreme that they name: `scan_offsets`: position s of a device's tile has row offset in [0, 256) and column offset in [s * 128, (s + 1) * 128).
All inputs are finite; a program needn't handle non-finite values.
Results may differ from a plain program's by a relative error of at most 0.002.
The roundings to bfloat16 on the way count: a program that leaves them out, or rounds other values in their place, can miss the bound.
Values may be sent and summed in bfloat16 or wider, within the bound.
A program may use at most 128 MiB of HBM per device.

v0:
```python
import math

import jax
import jax.numpy as jnp
from jax import lax
from jax.sharding import PartitionSpec as P


def passed_along(value, axis, steps):
    count = lax.axis_size(axis)
    pairs = [(source, (source + steps) % count) for source in range(count)]
    return lax.ppermute(value, axis, pairs)


def dft_tables(size):
    index = jnp.arange(size, dtype=jnp.int32)
    wrapped = index[:, None] * index[None, :] % size
    angle = wrapped.astype(jnp.float32) * (2.0 * math.pi / size)
    norm = 1.0 / math.sqrt(size)
    return (
        (jnp.cos(angle) * norm).astype(jnp.bfloat16),
        (-jnp.sin(angle) * norm).astype(jnp.bfloat16),
    )


def left_apply(stacked, wave, conjugate):
    size = wave.shape[-1]
    product = jnp.einsum("aj,psjk->psak", stacked, wave, preferred_element_type=jnp.float32)
    cos_real = product[0, :, :size]
    sin_real = product[0, :, size:]
    cos_imag = product[1, :, :size]
    sin_imag = product[1, :, size:]
    if conjugate:
        return jnp.stack([cos_real + sin_imag, cos_imag - sin_real])
    return jnp.stack([cos_real - sin_imag, cos_imag + sin_real])


def right_apply(wave, paired, conjugate):
    size = wave.shape[-1]
    product = jnp.einsum("psjk,kb->psjb", wave, paired, preferred_element_type=jnp.float32)
    real_cos = product[0, :, :, :size]
    real_sin = product[0, :, :, size:]
    imag_cos = product[1, :, :, :size]
    imag_sin = product[1, :, :, size:]
    if conjugate:
        return jnp.stack([real_cos + imag_sin, imag_cos - real_sin])
    return jnp.stack([real_cos - imag_sin, real_sin + imag_cos])


def shards(measured, module_row, scan_offsets, specimen, illumination):
    slots = scan_offsets.shape[2]
    size = illumination.shape[-1]
    tile_rows = specimen.shape[1]
    tile_cols = specimen.shape[2]
    arrived = lax.all_to_all(measured, "row", split_axis=0, concat_axis=1, tiled=True)
    modules = arrived.shape[1]
    inverse = (
        jnp.zeros((modules,), jnp.int32).at[module_row].set(jnp.arange(modules, dtype=jnp.int32))
    )
    amplitude = jnp.take(arrived, inverse, axis=1).reshape(slots, size, size)
    right = passed_along(specimen, "col", -1)
    band = jnp.concatenate([specimen, right], axis=2)
    below = passed_along(band, "row", -1)
    farther = passed_along(band, "row", -2)
    region = jnp.concatenate([band, below, farther], axis=1)
    zero = jnp.zeros((), jnp.int32)
    starts = [
        (zero, scan_offsets[0, 0, slot, 0], scan_offsets[0, 0, slot, 1]) for slot in range(slots)
    ]
    patches = jnp.stack(
        [lax.dynamic_slice(region, starts[slot], (2, size, size)) for slot in range(slots)], axis=1
    )
    ill_real = illumination[0][None]
    ill_imag = illumination[1][None]
    spec_real = patches[0]
    spec_imag = patches[1]
    wave = jnp.stack(
        [ill_real * spec_real - ill_imag * spec_imag, ill_real * spec_imag + ill_imag * spec_real]
    ).astype(jnp.bfloat16)
    cos_table, sin_table = dft_tables(size)
    stacked = jnp.concatenate([cos_table, sin_table], axis=0)
    paired = jnp.concatenate([cos_table, sin_table], axis=1)
    half = left_apply(stacked, wave, False).astype(jnp.bfloat16)
    far_field = right_apply(half, paired, False)
    magnitude = jnp.sqrt(far_field[0] * far_field[0] + far_field[1] * far_field[1])
    factor = amplitude.astype(jnp.float32) / jnp.maximum(magnitude, 0.25) - 1.0
    correction = (factor[None] * far_field).astype(jnp.bfloat16)
    back_half = left_apply(stacked, correction, True).astype(jnp.bfloat16)
    exit_change = right_apply(back_half, paired, True)
    chg_real = exit_change[0]
    chg_imag = exit_change[1]
    patch_grads = jnp.stack(
        [ill_real * chg_real + ill_imag * chg_imag, ill_real * chg_imag - ill_imag * chg_real]
    )
    num_real = jnp.sum(spec_real * chg_real + spec_imag * chg_imag, axis=0)
    num_imag = jnp.sum(spec_real * chg_imag - spec_imag * chg_real, axis=0)
    density = jnp.sum(spec_real * spec_real + spec_imag * spec_imag, axis=0)
    accum = jnp.zeros_like(region)
    for slot in range(slots):
        current = lax.dynamic_slice(accum, starts[slot], (2, size, size))
        accum = lax.dynamic_update_slice(accum, current + patch_grads[:, slot], starts[slot])
    upper = accum[:, :tile_rows]
    middle = accum[:, tile_rows : 2 * tile_rows]
    lower = accum[:, 2 * tile_rows :]
    rows_summed = upper + passed_along(middle, "row", 1) + passed_along(lower, "row", 2)
    specimen_step = rows_summed[:, :, :tile_cols] + passed_along(
        rows_summed[:, :, tile_cols:], "col", 1
    )
    totals = lax.psum((num_real, num_imag, density), ("row", "col"))
    root = jnp.sqrt(totals[2] + 1e-06)
    illumination_step = jnp.stack([totals[0] / root, totals[1] / root])
    return (specimen_step, illumination_step)


def solution(mesh):
    return jax.shard_map(
        shards,
        mesh=mesh,
        in_specs=(
            P("col", "row", None, None),
            P(),
            P("row", "col", None, None),
            P(None, "row", "col"),
            P(),
        ),
        out_specs=(P(None, "row", "col"), P()),
        check_vma=False,
    )
```

profile of v0, /device:TPU:0, one launch (start us, length us, event | category | flops | bytes accessed | tf_op | source)
XLA Modules:
  0.0 496.6 jit_solution(17110034591982727380)
XLA Ops:
  11.9 10.3 %collective-permute-done = f32[2,256,512]{2,1,0:T(8,128)S(1)} collective-permute-done((f32[2,256,512]{2,1,0:T(8,128)}, f32[2,256,512]{2,1,0:T(8,128)S(1)}, u32[]{:S(2)}, u32[]{:S(2)}) %collective-permute-start) | collective-permute-done | bytes 1048608 | tf_op jit(solution)/shard_map/ppermute | solution.py:12
  23.3 4.5 collective-permute-start.1
  28.3 4.4 all-to-all-start
  52.3 5.3 %multiply_convert_fusion = (bf16[512,512]{1,0:T(8,128)(2,1)S(1)}, bf16[512,512]{1,0:T(8,128)(2,1)}) fusion(), kind=kLoop, calls=%fused_computation.72 | loop fusion | flops 4980736 | bytes 1048576 | tf_op jit(solution)/shard_map/convert_element_type | solution.py:22
  57.6 16.6 %collective-permute-done.1 = f32[2,256,1024]{2,1,0:T(8,128)} collective-permute-done((f32[2,256,1024]{2,1,0:T(8,128)}, f32[2,256,1024]{2,1,0:T(8,128)}, u32[]{:S(2)}, u32[]{:S(2)}) %collective-permute-start.1) | collective-permute-done | bytes 2097184 | tf_op jit(solution)/shard_map/ppermute | solution.py:12
  74.2 44.9 %collective-permute-done.2 = f32[2,256,1024]{2,1,0:T(8,128)} collective-permute-done((f32[2,256,1024]{2,1,0:T(8,128)}, f32[2,256,1024]{2,1,0:T(8,128)}, u32[]{:S(2)}, u32[]{:S(2)}) %collective-permute-start.2) | collective-permute-done | bytes 2097184 | tf_op jit(solution)/shard_map/ppermute | solution.py:12
  119.2 3.4 pad_maximum_fusion.1
  122.6 5.7 %constant_dynamic-slice_fusion.3 = (f32[2,512,512]{2,1,0:T(8,128)}, f32[2,512,512]{2,1,0:T(8,128)}, f32[2,512,512]{2,1,0:T(8,128)}, f32[2,512,512]{2,1,0:T(8,128)}) fusion(f32[2,768,1024]{2,1,0:T(8,128)S(1)} %pad_maximum_fusion.1, s32[]{:T(128)S(6)} %select_n.74, s32[]{:T(128)S(6)} %select_n.75, s32[]{:T(128)S(6)} %select_n.80, s32[]{:T(128)S(6)} %select_n.81, ...), kind=kLoop, calls=%fused_computation.88 | loop fusion | bytes 16777248 | tf_op jit(solution)/shard_map/dynamic_slice | solution.py:71
  134.1 3.0 copy.67
  140.0 3.9 pad_maximum_fusion
  147.4 4.6 convolution_bitcast_fusion.1
  153.5 8.4 %fusion.9 = f32[2,4,512,1024]{3,2,1,0:T(8,128)} fusion(bf16[1,4,512,512]{2,3,1,0:T(8,128)(2,1)S(1)} %get-tuple-element.24, bf16[1,4,512,512]{2,3,1,0:T(8,128)(2,1)S(1)} %get-tuple-element.23, bf16[512,512]{1,0:T(8,128)(2,1)S(1)} %get-tuple-element.47, bf16[512,512]{1,0:T(8,128)(2,1)S(1)} %copy-done.5), kind=kOutput, calls=%fused_computation.29 | convolution fusion | flops 4299161600 | bytes 22020096 | tf_op jit(solution)/shard_map/psjk,kb->psjb/dot_general | solution.py:40
  163.8 3.2 copy.62
  167.0 3.7 gather_fusion
  172.4 7.8 %add_bitcast_fusion = (f32[4,512,512]{2,1,0:T(8,128)S(1)}, f32[1,4,512,512]{3,2,1,0:T(8,128)S(1)}, f32[1,4,512,512]{3,2,1,0:T(8,128)S(1)}) fusion(bf16[1,4,512,512]{3,2,1,0:T(8,128)(2,1)S(1)} %bitcast.66, pred[512]{0:T(512)(128)(4,1)S(1)} %broadcast_in_dim.28, f32[2,4,512,1024]{3,2,1,0:T(8,128)} %fusion.9), kind=kLoop, calls=%fused_computation.43 | loop fusion | flops 10485760 | bytes 31457792 | tf_op jit(solution)/shard_map/mul | solution.py:87
  180.3 9.3 %convolution_bitcast_fusion = f32[2,4,1024,512]{2,3,1,0:T(8,128)} fusion(f32[1,4,512,512]{3,2,1,0:T(8,128)S(1)} %get-tuple-element.20, f32[1,4,512,512]{3,2,1,0:T(8,128)S(1)} %get-tuple-element.19, f32[4,512,512]{2,1,0:T(8,128)S(1)} %get-tuple-element.18, bf16[512,512]{1,0:T(8,128)(2,1)S(1)} %get-tuple-element.47, bf16[512,512]{1,0:T(8,128)(2,1)} %get-tuple-element.48), kind=kOutput, calls=%fused_computation.11 | convolution fusion | flops 4303355904 | bytes 30408704 | tf_op jit(solution)/shard_map/aj,psjk->psak/dot_general | solution.py:28
  189.6 6.8 %fusion.3 = (bf16[1,4,512,512]{2,3,1,0:T(8,128)(2,1)S(1)}, bf16[1,4,512,512]{2,3,1,0:T(8,128)(2,1)S(1)}) fusion(f32[2,4,1024,512]{2,3,1,0:T(8,128)} %convolution_bitcast_fusion), kind=kLoop, calls=%fused_computation.19 | loop fusion | flops 4194304 | bytes 20971520 | tf_op jit(solution)/shard_map/convert
  196.4 8.3 %fusion.13 = f32[2,4,512,1024]{2,3,1,0:T(8,128)} fusion(bf16[1,4,512,512]{2,3,1,0:T(8,128)(2,1)S(1)} %get-tuple-element.22, bf16[1,4,512,512]{2,3,1,0:T(8,128)(2,1)S(1)} %get-tuple-element.21, bf16[512,512]{1,0:T(8,128)(2,1)S(1)} %get-tuple-element.47, bf16[512,512]{1,0:T(8,128)(2,1)S(1)} %copy-done.6), kind=kOutput, calls=%fused_computation.33 | convolution fusion | flops 4299161600 | bytes 22020096 | tf_op jit(solution)/shard_map/psjk,kb->psjb/dot_general | solution.py:40
  204.7 11.0 %add_reduce_fusion.1 = (f32[512,512]{0,1:T(8,128)}, f32[512,512]{0,1:T(8,128)}, f32[512,512]{0,1:T(8,128)}, f32[1,4,512,512]{2,3,1,0:T(8,128)S(1)}, f32[1,4,512,512]{2,3,1,0:T(8,128)}) fusion(f32[2,4,512,512]{2,3,1,0:T(8,128)S(1)} %bitcast.65, f32[2,4,512,1024]{2,3,1,0:T(8,128)} %fusion.13), kind=kLoop, calls=%fused_computation.39 | loop fusion | flops 13893632 | bytes 36700160 | tf_op jit(solution)/shard_map/reduce_sum | solution.py:95
  215.8 3.7 multiply_subtract_fusion
  222.8 3.1 broadcast_in_dim.25
  225.9 14.1 %dynamic_update_slice.12 = f32[2,768,1024]{1,2,0:T(8,128)} dynamic-update-slice(f32[2,768,1024]{1,2,0:T(8,128)} %broadcast_in_dim.25, f32[2,512,512]{1,2,0:T(8,128)S(1)} %fusion.22, s32[]{:T(128)} %constant.16.clone.1, s32[]{:T(128)S(6)} %select_n.74, s32[]{:T(128)S(6)} %select_n.75) | dynamic-update-slice | bytes 4194308 | tf_op jit(solution)/shard_map/dynamic_update_slice | solution.py:101
  240.0 3.0 fusion.25
  243.0 14.3 %dynamic_update_slice.13 = f32[2,768,1024]{1,2,0:T(8,128)} dynamic-update-slice(f32[2,768,1024]{1,2,0:T(8,128)} %dynamic_update_slice.12, f32[2,512,512]{1,2,0:T(8,128)S(1)} %fusion.25, s32[]{:T(128)} %constant.16.clone.1, s32[]{:T(128)S(6)} %select_n.76, s32[]{:T(128)S(6)} %select_n.77) | dynamic-update-slice | bytes 4194308 | tf_op jit(solution)/shard_map/dynamic_update_slice | solution.py:101
  257.3 3.0 fusion.20
  260.3 14.3 %dynamic_update_slice.14 = f32[2,768,1024]{1,2,0:T(8,128)} dynamic-update-slice(f32[2,768,1024]{1,2,0:T(8,128)} %dynamic_update_slice.13, f32[2,512,512]{1,2,0:T(8,128)S(1)} %fusion.20, s32[]{:T(128)} %constant.16.clone.1, s32[]{:T(128)S(6)} %select_n.78, s32[]{:T(128)S(6)} %select_n.79) | dynamic-update-slice | bytes 4194308 | tf_op jit(solution)/shard_map/dynamic_update_slice | solution.py:101
  274.6 3.0 fusion.28
  277.7 13.7 %dynamic_update_slice.15 = f32[2,768,1024]{1,2,0:T(8,128)} dynamic-update-slice(f32[2,768,1024]{1,2,0:T(8,128)} %dynamic_update_slice.14, f32[2,512,512]{1,2,0:T(8,128)S(1)} %fusion.28, s32[]{:T(128)} %constant.16.clone.1, s32[]{:T(128)S(6)} %select_n.80, s32[]{:T(128)S(6)} %select_n.81) | dynamic-update-slice | bytes 4194308 | tf_op jit(solution)/shard_map/dynamic_update_slice | solution.py:101
  291.3 4.7 fusion.42
  298.1 67.3 %collective-permute-done.3 = f32[2,256,1024]{1,2,0:T(8,128)S(1)} collective-permute-done((f32[2,256,1024]{1,2,0:T(8,128)}, f32[2,256,1024]{1,2,0:T(8,128)S(1)}, u32[]{:S(2)}, u32[]{:S(2)}) %collective-permute-start.3) | collective-permute-done | bytes 2097184 | tf_op jit(solution)/shard_map/ppermute | solution.py:12
  366.7 3.3 fusion.26
  370.2 110.2 %all-reduce.3.cloned.1.call-done = (f32[512,512]{0,1:T(8,128)}, f32[512,512]{0,1:T(8,128)}, f32[512,512]{0,1:T(8,128)}) async-done(((f32[512,512]{0,1:T(8,128)}, f32[512,512]{0,1:T(8,128)}, f32[512,512]{0,1:T(8,128)}), (f32[512,512]{0,1:T(8,128)}, f32[512,512]{0,1:T(8,128)}, f32[512,512]{0,1:T(8,128)})) %all-reduce.3.cloned.1.call-update) | async-done | bytes 3145744 | tf_op jit(solution)/shard_map/psum | solution.py:109
  (64 shorter events, 44.4 us)
Async XLA Ops:
  7.2 25.5 %copy-start.10 = (s32[32]{0:T(128)S(1)}, s32[32]{0:T(128)}, u32[]{:S(2)}) copy-start(s32[32]{0:T(128)} %param.6) | copy-start | bytes 388
  7.2 26.3 %copy-start.7 = (f32[2,512,512]{2,1,0:T(8,128)S(1)}, f32[2,512,512]{2,1,0:T(8,128)}, u32[]{:S(2)}) copy-start(f32[2,512,512]{2,1,0:T(8,128)} %param.9) | copy-start | bytes 6291460
  7.2 15.1 %collective-permute-start = (f32[2,256,512]{2,1,0:T(8,128)}, f32[2,256,512]{2,1,0:T(8,128)S(1)}, u32[]{:S(2)}, u32[]{:S(2)}) collective-permute-start(f32[2,256,512]{2,1,0:T(8,128)} %param.8), channel_id=1, source_target_pairs={{0,3},{1,0},{2,1},{3,2},{4,7},{5,4},{6,5},{7,6},{8,11},{9,8},{10,9... | collective-permute-start | bytes 3145736 | tf_op jit(solution)/shard_map/ppermute | solution.py:12
  23.3 11.3 %copy-start.9 = (s32[1,1,4,2]{2,3,1,0:T(2,128)S(1)}, s32[1,1,4,2]{2,3,1,0:T(2,128)}, u32[]{:S(2)}) copy-start(s32[1,1,4,2]{2,3,1,0:T(2,128)} %param.7) | copy-start | bytes 100
  23.3 50.9 %collective-permute-start.1 = (f32[2,256,1024]{2,1,0:T(8,128)}, f32[2,256,1024]{2,1,0:T(8,128)}, u32[]{:S(2)}, u32[]{:S(2)}) collective-permute-start(f32[2,256,1024]{2,1,0:T(8,128)} %constant_dynamic-update-slice_fusion), channel_id=1, source_target_pairs={{0,28},{4,0},{8,4},{12,8},{16,12},{20,16},{24,20},{28,24},{1,29},{... | collective-permute-start | bytes 6291464 | tf_op jit(solution)/shard_map/ppermute | solution.py:12
  27.8 91.3 %collective-permute-start.2 = (f32[2,256,1024]{2,1,0:T(8,128)}, f32[2,256,1024]{2,1,0:T(8,128)}, u32[]{:S(2)}, u32[]{:S(2)}) collective-permute-start(f32[2,256,1024]{2,1,0:T(8,128)} %constant_dynamic-update-slice_fusion), channel_id=1, source_target_pairs={{0,24},{4,28},{8,0},{12,4},{16,8},{20,12},{24,16},{28,20},{1,25},{... | collective-permute-start | bytes 6291464 | tf_op jit(solution)/shard_map/ppermute | solution.py:12
  28.3 135.5 %all-to-all-start = ((bf16[32,4,16,512]{3,2,1,0:T(8,128)(2,1)}), bf16[32,4,16,512]{3,2,1,0:T(8,128)(2,1)}, u32[]{:S(2)}, u32[]{:S(2)}) async-start(bf16[32,4,16,512]{3,2,1,0:T(8,128)(2,1)} %param.5), calls=%async_computation | async-start | bytes 4194304 | tf_op jit(solution)/shard_map/all_to_all | solution.py:55
  32.7 447.7 %all-reduce.3.cloned.1.call-start = ((), (), s32[]{:S(2)}) async-start(), calls=%async_computation.1 | async-start | bytes 6291456 | tf_op jit(solution)/shard_map/psum | solution.py:109
  47.1 96.7 %copy-start.3 = (f32[512,512]{0,1:T(8,128)}, f32[512,512]{0,1:T(8,128)S(1)}, u32[]{:S(2)}) copy-start(f32[512,512]{0,1:T(8,128)S(1)} %copy.68) | copy-start | bytes 3145732
  143.9 3.5 copy-start.2
  143.9 3.5 copy-start.5
  189.6 6.8 %copy-start.6 = (bf16[512,512]{1,0:T(8,128)(2,1)S(1)}, bf16[512,512]{1,0:T(8,128)(2,1)}, u32[]{:S(2)}) copy-start(bf16[512,512]{1,0:T(8,128)(2,1)} %get-tuple-element.48) | copy-start | bytes 1572868
  189.6 15.2 %slice-start = ((s8[8388608]{0:T(1024)(128)(4,1)}), s8[4194304]{0:T(1024)(128)(4,1)S(1)}, s32[]{:S(2)}) async-start(s8[8388608]{0:T(1024)(128)(4,1)} %bitcast.64), calls=%async_computation.2 | async-start | bytes 8388608
  196.4 8.4 %slice-start.1 = ((s8[8388608]{0:T(1024)(128)(4,1)}), s8[4194304]{0:T(1024)(128)(4,1)S(1)}, s32[]{:S(2)}) async-start(s8[8388608]{0:T(1024)(128)(4,1)} %bitcast.64), calls=%async_computation.3 | async-start | bytes 8388608
  204.7 11.0 %copy-start.4 = (f32[512,512]{0,1:T(8,128)S(1)}, f32[512,512]{0,1:T(8,128)}, u32[]{:S(2)}) copy-start(f32[512,512]{0,1:T(8,128)} %copy-done.3) | copy-start | bytes 3145732
  219.5 2.1 copy-start
  219.5 3.3 copy-start.1
  296.0 69.4 %collective-permute-start.3 = (f32[2,256,1024]{1,2,0:T(8,128)}, f32[2,256,1024]{1,2,0:T(8,128)S(1)}, u32[]{:S(2)}, u32[]{:S(2)}) collective-permute-start(f32[2,256,1024]{1,2,0:T(8,128)} %get-tuple-element.29), channel_id=1, source_target_pairs={{0,4},{4,8},{8,12},{12,16},{16,20},{20,24},{24,28},{28,0},{1,5},{5... | collective-permute-start | bytes 6291464 | tf_op jit(solution)/shard_map/ppermute | solution.py:12
  296.0 70.7 %collective-permute-start.4 = (f32[2,256,1024]{1,2,0:T(8,128)}, f32[2,256,1024]{1,2,0:T(8,128)}, u32[]{:S(2)}, u32[]{:S(2)}) collective-permute-start(f32[2,256,1024]{1,2,0:T(8,128)} %get-tuple-element.30), channel_id=1, source_target_pairs={{0,8},{4,12},{8,16},{12,20},{16,24},{20,28},{24,0},{28,4},{1,9},{5... | collective-permute-start | bytes 6291464 | tf_op jit(solution)/shard_map/ppermute | solution.py:12
  365.4 1.3 copy-start.8
  370.2 116.9 %collective-permute-start.5 = (f32[2,256,512]{1,2,0:T(8,128)S(1)}, f32[2,256,512]{1,2,0:T(8,128)}, u32[]{:S(2)}, u32[]{:S(2)}) collective-permute-start(f32[2,256,512]{1,2,0:T(8,128)S(1)} %slice.178), channel_id=1, source_target_pairs={{0,1},{1,2},{2,3},{3,0},{4,5},{5,6},{6,7},{7,4},{8,9},{9,10},{10,1... | collective-permute-start | bytes 3145736 | tf_op jit(solution)/shard_map/ppermute | solution.py:12
Sparse Core Ops, SparseCore 0:
  298.2 182.1 all-reduce.2
where the time goes:
time: 499 us; the launch traced here: 497 us
  waiting for transfers between devices  251 us (50%)
  local copies, waits for them, and re-layouts  109 us (22%)
  other arithmetic  62.8 us (13%)
  matrix products  30.6 us (6%)
  between operations  29.3 us (6%)
  starting transfers between devices  13.9 us (3%)
    ppermute x6, waiting for transfers between devices, passed_along(): return lax.ppermute(value, axis, pairs)  139 us
    psum x1, waiting for transfers between devices, shards(): totals = lax.psum((num_real, num_imag, density), ('row', 'col'))  110 us
    dynamic_update_slice x4, local copies, waits for them, and re-layouts, shards(): lax.dynamic_update_slice(accum, current + patch_grads[:, slot], starts[sl...  56.3 us
    dynamic_slice x5, local copies, waits for them, and re-layouts, shards(): lax.dynamic_slice(region, starts[slot], (2, size, size))  17.4 us
    dot_general x2, matrix products, right_apply(): jnp.einsum('psjk,kb->psjb', wave, paired, preferred_element_type=jnp.floa...  16.7 us
    dot_general x2, matrix products, left_apply(): jnp.einsum('aj,psjk->psak', stacked, wave, preferred_element_type=jnp.flo...  13.9 us
    unnamed x29, local copies, waits for them, and re-layouts  12.8 us
    reduce_sum x1, other arithmetic, shards(): num_real = jnp.sum(spec_real * chg_real + spec_imag * chg_imag, axis=0)  11 us
  transfers between devices with their start and end apart: 8, of which 6 were waited for; matrix products, arithmetic and copies ran while one was open for 13% of the time, Pallas kernels for 0%

commit v1 on v0

v1 whole, which is shorter than its diff:
```python
import functools
import math

import jax
import jax.numpy as jnp
from jax import lax
from jax.experimental import pallas as pl
from jax.experimental.pallas import tpu as pltpu
from jax.sharding import PartitionSpec as P

VMEM_LIMIT = 56 * 2**20
LANES = 128
SUBLANES = 8


def passed_along(value, axis, steps):
    count = lax.axis_size(axis)
    pairs = [(source, (source + steps) % count) for source in range(count)]
    return lax.ppermute(value, axis, pairs)


def dft_tables(size):
    index = jnp.arange(size, dtype=jnp.int32)
    wrapped = index[:, None] * index[None, :] % size
    angle = wrapped.astype(jnp.float32) * (2.0 * math.pi / size)
    norm = 1.0 / math.sqrt(size)
    return (
        (jnp.cos(angle) * norm).astype(jnp.bfloat16),
        (-jnp.sin(angle) * norm).astype(jnp.bfloat16),
    )


def mdot(left, right):
    return jnp.dot(left, right, preferred_element_type=jnp.float32)


def forward_kernel(
    offsets, t00, t01, t10, t11, t20, t21, ill, left, right, far, patch, density, region, wave, half, sems
):
    slot = pl.program_id(0)
    size = ill.shape[-1]
    rows, cols = t00.shape[1:]
    wide = size + LANES
    step = 64

    @pl.when(slot == 0)
    def _():
        copies = []
        for at, tile in enumerate((t00, t01, t10, t11, t20, t21)):
            down, across = divmod(at, 2)
            place = region.at[:, pl.ds(down * rows, rows), pl.ds(across * cols, cols)]
            copies.append(pltpu.make_async_copy(tile, place, sems.at[at]))
        for copy in copies:
            copy.start()
        for copy in copies:
            copy.wait()
        density[...] = jnp.zeros_like(density)

    row_at = offsets[slot, 0]
    fine = lax.rem(row_at, SUBLANES)
    coarse = row_at - fine
    tall = step + SUBLANES
    base = pl.multiple_of(slot * (cols // pl.num_programs(0)), LANES)
    shift = lax.rem(wide - (offsets[slot, 1] - base), wide)
    raised = lax.rem(tall - fine, tall)

    def gather(i, carry):
        at = pl.multiple_of(i * step, step)
        here = pl.ds(at, step)
        parts = []
        for part in range(2):
            top = pl.multiple_of(coarse + at, SUBLANES)
            block = region[part, pl.ds(top, tall), pl.ds(base, wide)]
            moved = pltpu.roll(block, shift, 1)[:, :size]
            parts.append(pltpu.roll(moved, raised, 0)[:step])
        real, imag = parts
        patch[0, 0, here, :] = real
        patch[0, 1, here, :] = imag
        density[here, :] += real * real + imag * imag
        ill_real = ill[0, here, :]
        ill_imag = ill[1, here, :]
        wave[here, :] = (ill_real * real - ill_imag * imag).astype(jnp.bfloat16)
        low = pl.ds(pl.multiple_of(size + at, step), step)
        wave[low, :] = (ill_real * imag + ill_imag * real).astype(jnp.bfloat16)
        return carry

    lax.fori_loop(0, size // step, gather, 0)
    half[:, :size] = mdot(left[:size, :], wave[...]).astype(jnp.bfloat16)
    half[:, size:] = mdot(left[size:, :], wave[...]).astype(jnp.bfloat16)
    far[0] = mdot(half[...], right[...])


def backward_kernel(
    offsets, module_row, amp, far, patch, ill, left, right, upper, middle, lower, side, numer,
    frame, accum, corr, back, change,
):
    slot = pl.program_id(0)
    size = ill.shape[-1]
    rows, cols = upper.shape[1:]
    wide = size + LANES
    step = 64
    senders, _, own, depth, _ = amp.shape

    @pl.when(slot == 0)
    def _():
        accum[...] = jnp.zeros_like(accum)
        numer[...] = jnp.zeros_like(numer)

    for sender in range(senders):
        for at in range(own):
            top = pl.multiple_of(module_row[sender * own + at] * depth, depth)
            frame[pl.ds(top, depth), :] = amp[sender, 0, at]

    def correct(i, carry):
        at = pl.multiple_of(i * step, step)
        here = pl.ds(at, step)
        real = far[0, here, :size]
        imag = far[0, here, size:]
        magnitude = jnp.sqrt(real * real + imag * imag)
        factor = frame[here, :].astype(jnp.float32) / jnp.maximum(magnitude, 0.25) - 1.0
        corr[here, :] = (factor * real).astype(jnp.bfloat16)
        low = pl.ds(pl.multiple_of(size + at, step), step)
        corr[low, :] = (factor * imag).astype(jnp.bfloat16)
        return carry

    lax.fori_loop(0, size // step, correct, 0)
    back[:, :size] = mdot(right[:size, :], corr[...]).astype(jnp.bfloat16)
    back[:, size:] = mdot(right[size:, :], corr[...]).astype(jnp.bfloat16)
    change[...] = mdot(back[...], left[...])

    row_at = offsets[slot, 0]
    fine = lax.rem(row_at, SUBLANES)
    coarse = row_at - fine
    tall = step + SUBLANES
    base = pl.multiple_of(slot * (cols // pl.num_programs(0)), LANES)
    shift = offsets[slot, 1] - base
    blank_below = jnp.zeros((SUBLANES, size), jnp.float32)
    blank_beside = jnp.zeros((tall, LANES), jnp.float32)

    def spread(i, carry):
        at = pl.multiple_of(i * step, step)
        here = pl.ds(at, step)
        chg_real = change[here, :size]
        chg_imag = change[here, size:]
        ill_real = ill[0, here, :]
        ill_imag = ill[1, here, :]
        real = patch[0, 0, here, :]
        imag = patch[0, 1, here, :]
        numer[0, here, :] += real * chg_real + imag * chg_imag
        numer[1, here, :] += real * chg_imag - imag * chg_real
        grads = (
            ill_real * chg_real + ill_imag * chg_imag,
            ill_real * chg_imag - ill_imag * chg_real,
        )
        for part in range(2):
            moved = pltpu.roll(jnp.concatenate([grads[part], blank_below], axis=0), fine, 0)
            moved = pltpu.roll(jnp.concatenate([moved, blank_beside], axis=1), shift, 1)
            top = pl.multiple_of(coarse + at, SUBLANES)
            accum[part, pl.ds(top, tall), pl.ds(base, wide)] += moved
        return carry

    lax.fori_loop(0, size // step, spread, 0)

    @pl.when(slot == pl.num_programs(0) - 1)
    def _():
        upper[...] = accum[:, :rows, :cols]
        middle[...] = accum[:, rows : 2 * rows, :cols]
        lower[...] = accum[:, 2 * rows :, :cols]
        side[...] = accum[:, :, cols:]


def whole():
    return pl.BlockSpec(memory_space=pltpu.VMEM)


def forward(offsets, tiles, ill, left, right):
    slots = offsets.shape[0]
    size = ill.shape[-1]
    rows, cols = tiles[0].shape[1:]
    return pl.pallas_call(
        forward_kernel,
        grid=(slots,),
        in_specs=[pl.BlockSpec(memory_space=pltpu.SMEM)]
        + [pl.BlockSpec(memory_space=pl.ANY)] * 6
        + [whole()] * 3,
        out_specs=[
            pl.BlockSpec((1, size, 2 * size), lambda s: (s, 0, 0)),
            pl.BlockSpec((1, 2, size, size), lambda s: (s, 0, 0, 0)),
            pl.BlockSpec((size, size), lambda s: (0, 0)),
        ],
        out_shape=[
            jax.ShapeDtypeStruct((slots, size, 2 * size), jnp.float32),
            jax.ShapeDtypeStruct((slots, 2, size, size), jnp.float32),
            jax.ShapeDtypeStruct((size, size), jnp.float32),
        ],
        scratch_shapes=[
            pltpu.VMEM((2, 3 * rows, 2 * cols), jnp.float32),
            pltpu.VMEM((2 * size, size), jnp.bfloat16),
            pltpu.VMEM((size, 2 * size), jnp.bfloat16),
            pltpu.SemaphoreType.DMA((6,)),
        ],
        compiler_params=pltpu.CompilerParams(vmem_limit_bytes=VMEM_LIMIT),
        cost_estimate=pl.CostEstimate(
            flops=16 * slots * size**3, bytes_accessed=28 * 2**20, transcendentals=0
        ),
        name="forward",
    )(offsets, *tiles, ill, left, right)


def backward(offsets, module_row, amp, far, patch, ill, left, right, rows, cols):
    slots = offsets.shape[0]
    size = ill.shape[-1]
    senders, _, own, depth, _ = amp.shape
    scalar = pl.BlockSpec(memory_space=pltpu.SMEM)
    tile = jax.ShapeDtypeStruct((2, rows, cols), jnp.float32)
    return pl.pallas_call(
        backward_kernel,
        grid=(slots,),
        in_specs=[
            scalar,
            scalar,
            pl.BlockSpec((senders, 1, own, depth, size), lambda s: (0, s, 0, 0, 0)),
            pl.BlockSpec((1, size, 2 * size), lambda s: (s, 0, 0)),
            pl.BlockSpec((1, 2, size, size), lambda s: (s, 0, 0, 0)),
            whole(),
            whole(),
            whole(),
        ],
        out_specs=[whole()] * 5,
        out_shape=[
            tile,
            tile,
            tile,
            jax.ShapeDtypeStruct((2, 3 * rows, cols), jnp.float32),
            jax.ShapeDtypeStruct((2, size, size), jnp.float32),
        ],
        scratch_shapes=[
            pltpu.VMEM((size, size), jnp.bfloat16),
            pltpu.VMEM((2, 3 * rows, 2 * cols), jnp.float32),
            pltpu.VMEM((2 * size, size), jnp.bfloat16),
            pltpu.VMEM((size, 2 * size), jnp.bfloat16),
            pltpu.VMEM((size, 2 * size), jnp.float32),
        ],
        compiler_params=pltpu.CompilerParams(vmem_limit_bytes=VMEM_LIMIT),
        cost_estimate=pl.CostEstimate(
            flops=16 * slots * size**3, bytes_accessed=28 * 2**20, transcendentals=0
        ),
        name="backward",
    )(offsets, module_row, amp, far, patch, ill, left, right)


def shard_sum(value, devices):
    parts, size, width = value.shape
    cut = value.reshape(parts, devices, size // devices, width)
    got = lax.all_to_all(cut, ("row", "col"), split_axis=1, concat_axis=1, tiled=True)
    return jnp.sum(got, axis=1)


def shards(measured, module_row, scan_offsets, specimen, illumination):
    slots = scan_offsets.shape[2]
    size = illumination.shape[-1]
    rows, cols = specimen.shape[1:]
    n_row = lax.axis_size("row")
    devices = n_row * lax.axis_size("col")
    offsets = scan_offsets.reshape(slots, 2)
    below = passed_along(specimen, "row", -1)
    farther = passed_along(specimen, "row", -2)
    beside = passed_along(specimen, "col", -1)
    below_beside = passed_along(below, "col", -1)
    farther_beside = passed_along(farther, "col", -1)
    cut = measured.reshape((n_row, slots) + measured.shape[1:])
    amp = lax.all_to_all(cut, "row", split_axis=0, concat_axis=0, tiled=True)
    cos_table, sin_table = dft_tables(size)
    left = jnp.block([[cos_table, -sin_table], [sin_table, cos_table]])
    right = jnp.block([[cos_table, sin_table], [-sin_table, cos_table]])
    tiles = (specimen, beside, below, below_beside, farther, farther_beside)
    far, patch, density = forward(offsets, tiles, illumination, left, right)
    density_share = shard_sum(density[None], devices)
    upper, middle, lower, side, numer = backward(
        offsets, module_row, amp, far, patch, illumination, left, right, rows, cols
    )
    got = passed_along(side, "col", 1)
    middle = middle + got[:, rows : 2 * rows]
    lower = lower + got[:, 2 * rows :]
    specimen_step = (
        upper + got[:, :rows] + passed_along(middle, "row", 1) + passed_along(lower, "row", 2)
    )
    numer_share = shard_sum(numer, devices)
    share = numer_share / jnp.sqrt(density_share + 1e-06)
    illumination_step = lax.all_gather(share, ("row", "col"), axis=1, tiled=True)
    return (specimen_step, illumination_step)


def solution(mesh):
    return jax.shard_map(
        shards,
        mesh=mesh,
        in_specs=(
            P("col", "row", None, None),
            P(),
            P("row", "col", None, None),
            P(None, "row", "col"),
            P(),
        ),
        out_specs=(P(None, "row", "col"), P()),
        check_vma=False,
    )
```

time: 499 us -> 338 us (0.68)
  local copies, waits for them, and re-layouts: 109 us -> 6.95 us
  Pallas kernels: 0 us -> 57.3 us
  waiting for transfers between devices: 251 us -> 199 us
  other arithmetic: 62.8 us -> 24.4 us
  matrix products: 30.6 us -> 0 us
  starting transfers between devices: 13.9 us -> 36 us
  between operations: 29.3 us -> 14.1 us
    psum x1 -> x0, waiting for transfers between devices: 110 us -> none  [shards(): totals = lax.psum((num_real, num_imag, density), ('row', 'col'))]
    pallas_call x0 -> x2, Pallas kernels: none -> 57.3 us  [the longest x1 31 us: backward(): pl.pallas_call(backward_kernel, grid=(slots,), in_specs=[scalar, scalar,...]
    dynamic_update_slice x4 -> x0, local copies, waits for them, and re-layouts: 56.3 us -> none  [shards(): lax.dynamic_update_slice(accum, current + patch_grads[:, slot], starts[sl...]
    all_to_all x1 -> x3, waiting for transfers between devices: 1.88 us -> 48.3 us  [the longest x2 48.3 us: shard_sum(): lax.all_to_all(cut, ('row', 'col'), split_axis=1, concat_axis=1, tiled=True)]
    all_gather x0 -> x1, waiting for transfers between devices: none -> 35.9 us  [shards(): lax.all_gather(share, ('row', 'col'), axis=1, tiled=True)]
    dot_general x4 -> x0, matrix products: 30.6 us -> none  [the longest x2 16.7 us: right_apply(): jnp.einsum('psjk,kb->psjb', wave, paired, preferred_element_type=jnp.floa...]
    ppermute x6 -> x8, waiting for transfers between devices: 139 us -> 115 us  [passed_along(): return lax.ppermute(value, axis, pairs)]
    all_to_all x1 -> x3, starting transfers between devices: 4.36 us -> 27.4 us  [the longest x2 20 us: shard_sum(): lax.all_to_all(cut, ('row', 'col'), split_axis=1, concat_axis=1, tiled=True)]
  transfers between devices with their start and end apart: 8 -> 12, of which waited for: 6 -> 6; matrix products, arithmetic and copies ran while one was open for 13% -> 8% of each run, Pallas kernels for 0% -> 17%
where the time goes in v1:
time: 338 us
  waiting for transfers between devices  199 us (59%)
  Pallas kernels  57.3 us (17%)
  starting transfers between devices  36 us (11%)
  other arithmetic  24.4 us (7%)
  between operations  14.1 us (4%)
  local copies, waits for them, and re-layouts  6.95 us (2%)
    ppermute x8, waiting for transfers between devices, passed_along(): return lax.ppermute(value, axis, pairs)  115 us
    all_to_all x2, waiting for transfers between devices, shard_sum(): lax.all_to_all(cut, ('row', 'col'), split_axis=1, concat_axis=1, tiled=True)  48.3 us
    all_gather x1, waiting for transfers between devices, shards(): lax.all_gather(share, ('row', 'col'), axis=1, tiled=True)  35.9 us
    pallas_call x1, Pallas kernels, backward(): pl.pallas_call(backward_kernel, grid=(slots,), in_specs=[scalar, scalar,...  31 us
    pallas_call x1, Pallas kernels, forward(): pl.pallas_call(forward_kernel, grid=(slots,), in_specs=[pl.BlockSpec(memo...  26.2 us
    all_to_all x2, starting transfers between devices, shard_sum(): lax.all_to_all(cut, ('row', 'col'), split_axis=1, concat_axis=1, tiled=True)  20 us
    concatenate x1, other arithmetic, shards(): right = jnp.block([[cos_table, sin_table], [-sin_table, cos_table]])  10 us
    ppermute x8, starting transfers between devices, passed_along(): return lax.ppermute(value, axis, pairs)  8.57 us
  transfers between devices with their start and end apart: 12, of which 6 were waited for; matrix products, arithmetic and copies ran while one was open for 8% of the time, Pallas kernels for 17%

profile of v1, /device:TPU:0, one launch (start us, length us, event | category | flops | bytes accessed | tf_op | source)
XLA Modules:
  0.0 337.6 jit_solution(5496115763862415189)
XLA Ops:
  7.2 0.0 copy-start.4
  7.2 7.4 %all-to-all-start = ((bf16[8,4,4,16,512]{4,3,2,1,0:T(8,128)(2,1)}), bf16[8,4,4,16,512]{4,3,2,1,0:T(8,128)(2,1)S(1)}, u32[]{:S(2)}, u32[]{:S(2)}) async-start(bf16[8,4,4,16,512]{4,3,2,1,0:T(8,128)(2,1)} %bitcast.6), calls=%async_computation | async-start | bytes 4194304 | tf_op jit(solution)/shard_map/all_to_all | solution.py:272
  14.6 4.7 %collective-permute-start.1 = (f32[2,256,512]{2,1,0:T(8,128)S(1)}, f32[2,256,512]{2,1,0:T(8,128)}, u32[]{:S(2)}, u32[]{:S(2)}) collective-permute-start(f32[2,256,512]{2,1,0:T(8,128)S(1)} %copy-done.4), channel_id=1, source_target_pairs={{0,28},{4,0},{8,4},{12,8},{16,12},{20,16},{24,20},{28,24},{1,29},{... | collective-permute-start | bytes 3145736 | tf_op jit(solution)/shard_map/ppermute | solution.py:19
  19.3 0.6 collective-permute-start.3
  19.9 0.0 collective-permute-start
  19.9 53.3 %collective-permute-done.1.t10 = f32[2,256,512]{2,1,0:T(8,128)} collective-permute-done((f32[2,256,512]{2,1,0:T(8,128)S(1)}, f32[2,256,512]{2,1,0:T(8,128)}, u32[]{:S(2)}, u32[]{:S(2)}) %collective-permute-start.1) | collective-permute-done | bytes 1048608 | tf_op jit(solution)/shard_map/ppermute | solution.py:19
  73.2 22.6 %collective-permute-done.3.t20 = f32[2,256,512]{2,1,0:T(8,128)} collective-permute-done((f32[2,256,512]{2,1,0:T(8,128)S(1)}, f32[2,256,512]{2,1,0:T(8,128)}, u32[]{:S(2)}, u32[]{:S(2)}) %collective-permute-start.3) | collective-permute-done | bytes 1048608 | tf_op jit(solution)/shard_map/ppermute | solution.py:19
  95.7 0.6 copy.10.offsets
  96.4 4.0 %fusion.10 = bf16[512,512]{1,0:T(8,128)(2,1)S(1)} fusion(), kind=kLoop, calls=%fused_computation.22 | loop fusion | flops 5242880 | bytes 524288 | tf_op jit(solution)/shard_map/neg | solution.py:274
  100.4 4.4 %multiply_convert_fusion = (bf16[512,512]{1,0:T(8,128)(2,1)S(1)}, bf16[512,512]{1,0:T(8,128)(2,1)S(1)}) fusion(), kind=kLoop, calls=%fused_computation.17 | loop fusion | flops 4980736 | bytes 1048576 | tf_op jit(solution)/shard_map/convert_element_type | solution.py:29
  104.8 10.0 %fusion.1 = (bf16[1024,1024]{1,0:T(8,128)(2,1)}, bf16[1024,1024]{1,0:T(8,128)(2,1)}) fusion(bf16[512,512]{1,0:T(8,128)(2,1)S(1)} %get-tuple-element.23, bf16[512,512]{1,0:T(8,128)(2,1)S(1)} %fusion.10, bf16[512,512]{1,0:T(8,128)(2,1)S(1)} %get-tuple-element.22), kind=kLoop, calls=%fused_computation.5 | loop fusion | flops 14680064 | bytes 5767168 | tf_op jit(solution)/shard_map/jit(block)/concatenate | solution.py:275
  114.8 26.2 %forward.1 = (f32[4,512,1024]{2,1,0:T(8,128)}, f32[4,2,512,512]{3,2,1,0:T(8,128)}, f32[512,512]{1,0:T(8,128)}) custom-call(s32[4,2]{1,0:T(4,128)} %copy.10.offsets, f32[2,256,512]{2,1,0:T(8,128)} %t00.1, f32[2,256,512]{2,1,0:T(8,128)} %collective-permute-done.t01, f32[2,256,512]{2,1,0:T(8,128)} %collective-permute-done.1.t10, ...), custom_call_target="tpu_custom_call" | custom-call | flops 8589934592 | bytes 29360128 | tf_op jit(solution)/shard_map/forward/pallas_call | solution.py:180
  141.1 0.0 copy-start
  141.1 14.4 %all-to-all-start.2 = ((f32[1,32,16,512]{3,2,0,1:T(8,128)}), f32[1,32,16,512]{3,2,0,1:T(8,128)S(1)}, u32[]{:S(2)}, u32[]{:S(2)}) async-start(f32[1,32,16,512]{3,2,0,1:T(8,128)} %bitcast.8), calls=%async_computation.2 | async-start | bytes 2097152 | tf_op jit(solution)/shard_map/all_to_all | solution.py:255
  155.5 31.0 %backward.1 = (f32[2,256,512]{2,1,0:T(8,128)}, f32[2,256,512]{2,1,0:T(8,128)}, f32[2,256,512]{2,1,0:T(8,128)}, f32[2,768,512]{2,1,0:T(8,128)}, f32[2,512,512]{2,1,0:T(8,128)}) custom-call(s32[4,2]{1,0:T(4,128)} %copy.10.offsets, s32[32]{0:T(128)} %module_row.1, bf16[8,4,4,16,512]{4,3,2,1,0:T(8,128)(2,1)} %copy-done, f32[4,512,1024]{2,1,0:T(8,128)} %get-tuple-element.10.far, ...), custom_call_target="tpu_custom_call" | custom-call | flops 8589934592 | bytes 29360128 | tf_op jit(solution)/shard_map/backward/pallas_call | solution.py:216
  186.5 3.2 copy.11
  189.7 5.7 %all-to-all-start.1 = ((f32[2,32,16,512]{3,2,0,1:T(8,128)}), f32[2,32,16,512]{3,2,0,1:T(8,128)S(1)}, u32[]{:S(2)}, u32[]{:S(2)}) async-start(f32[2,32,16,512]{3,2,0,1:T(8,128)} %copy.11), calls=%async_computation.1 | async-start | bytes 4194304 | tf_op jit(solution)/shard_map/all_to_all | solution.py:255
  195.4 0.0 all-gather.2.cloned.1.call-start
  195.4 0.3 collective-permute-start.5
  195.7 0.1 reduce_sum.19
  195.8 48.3 %all-to-all-done.1 = f32[2,32,16,512]{3,2,0,1:T(8,128)S(1)} async-done(((f32[2,32,16,512]{3,2,0,1:T(8,128)}), f32[2,32,16,512]{3,2,0,1:T(8,128)S(1)}, u32[]{:S(2)}, u32[]{:S(2)}) %all-to-all-start.1) | async-done | bytes 2097184 | tf_op jit(solution)/shard_map/all_to_all | solution.py:255
  244.2 0.1 reduce_sum.18
  244.3 0.6 broadcast_divide_fusion
  244.9 0.0 all-gather.2.cloned.1.call-update
  245.0 9.6 %collective-permute-done.5 = f32[2,768,512]{2,1,0:T(8,128)} collective-permute-done((f32[2,768,512]{2,1,0:T(8,128)}, f32[2,768,512]{2,1,0:T(8,128)}, u32[]{:S(2)}, u32[]{:S(2)}) %collective-permute-start.5) | collective-permute-done | bytes 3145760 | tf_op jit(solution)/shard_map/ppermute | solution.py:19
  254.5 2.4 slice_add_fusion.1
  257.0 1.5 collective-permute-start.6
  258.5 1.5 collective-permute-start.7
  259.9 29.2 %collective-permute-done.6 = f32[2,256,512]{2,1,0:T(8,128)S(1)} collective-permute-done((f32[2,256,512]{2,1,0:T(8,128)S(1)}, f32[2,256,512]{2,1,0:T(8,128)S(1)}, u32[]{:S(2)}, u32[]{:S(2)}) %collective-permute-start.6) | collective-permute-done | bytes 1048608 | tf_op jit(solution)/shard_map/ppermute | solution.py:19
  289.1 2.7 fusion.6
  291.8 35.9 %all-gather.2.cloned.1.call-done = f32[2,512,512]{2,1,0:T(8,128)} async-done(((f32[2,16,512]{2,1,0:T(8,128)}), f32[2,512,512]{2,1,0:T(8,128)}) %all-gather.2.cloned.1.call-update) | async-done | bytes 2097168 | tf_op jit(solution)/shard_map/all_gather | solution.py:290
  327.7 3.1 copy.14
  (17 shorter events, 0.1 us)
Async XLA Ops:
  7.2 7.4 %copy-start.4 = (f32[2,256,512]{2,1,0:T(8,128)S(1)}, f32[2,256,512]{2,1,0:T(8,128)}, u32[]{:S(2)}) copy-start(f32[2,256,512]{2,1,0:T(8,128)} %t00.1) | copy-start | bytes 3145732
  7.2 88.6 %copy-start.3 = (s32[1,1,4,2]{2,3,1,0:T(2,128)S(1)}, s32[1,1,4,2]{2,3,1,0:T(2,128)}, u32[]{:S(2)}) copy-start(s32[1,1,4,2]{2,3,1,0:T(2,128)} %param.7) | copy-start | bytes 100
  7.2 133.9 %all-to-all-start = ((bf16[8,4,4,16,512]{4,3,2,1,0:T(8,128)(2,1)}), bf16[8,4,4,16,512]{4,3,2,1,0:T(8,128)(2,1)S(1)}, u32[]{:S(2)}, u32[]{:S(2)}) async-start(bf16[8,4,4,16,512]{4,3,2,1,0:T(8,128)(2,1)} %bitcast.6), calls=%async_computation | async-start | bytes 4194304 | tf_op jit(solution)/shard_map/all_to_all | solution.py:272
  14.6 58.6 %collective-permute-start.1 = (f32[2,256,512]{2,1,0:T(8,128)S(1)}, f32[2,256,512]{2,1,0:T(8,128)}, u32[]{:S(2)}, u32[]{:S(2)}) collective-permute-start(f32[2,256,512]{2,1,0:T(8,128)S(1)} %copy-done.4), channel_id=1, source_target_pairs={{0,28},{4,0},{8,4},{12,8},{16,12},{20,16},{24,20},{28,24},{1,29},{... | collective-permute-start | bytes 3145736 | tf_op jit(solution)/shard_map/ppermute | solution.py:19
  19.3 76.4 %collective-permute-start.3 = (f32[2,256,512]{2,1,0:T(8,128)S(1)}, f32[2,256,512]{2,1,0:T(8,128)}, u32[]{:S(2)}, u32[]{:S(2)}) collective-permute-start(f32[2,256,512]{2,1,0:T(8,128)S(1)} %copy-done.4), channel_id=1, source_target_pairs={{0,24},{4,28},{8,0},{12,4},{16,8},{20,12},{24,16},{28,20},{1,25},{... | collective-permute-start | bytes 3145736 | tf_op jit(solution)/shard_map/ppermute | solution.py:19
  19.9 94.9 %collective-permute-start = (f32[2,256,512]{2,1,0:T(8,128)S(1)}, f32[2,256,512]{2,1,0:T(8,128)}, u32[]{:S(2)}, u32[]{:S(2)}) collective-permute-start(f32[2,256,512]{2,1,0:T(8,128)S(1)} %copy-done.4), channel_id=1, source_target_pairs={{0,3},{1,0},{2,1},{3,2},{4,7},{5,4},{6,5},{7,6},{8,11},{9,8},{10,9... | collective-permute-start | bytes 3145736 | tf_op jit(solution)/shard_map/ppermute | solution.py:19
  73.2 41.7 %collective-permute-start.2 = (f32[2,256,512]{2,1,0:T(8,128)}, f32[2,256,512]{2,1,0:T(8,128)}, u32[]{:S(2)}, u32[]{:S(2)}) collective-permute-start(f32[2,256,512]{2,1,0:T(8,128)} %collective-permute-done.1.t10), channel_id=1, source_target_pairs={{0,3},{1,0},{2,1},{3,2},{4,7},{5,4},{6,5},{7,6},{8,11},{9,8},{10,9... | collective-permute-start | bytes 3145736 | tf_op jit(solution)/shard_map/ppermute | solution.py:19
  95.7 19.1 %collective-permute-start.4 = (f32[2,256,512]{2,1,0:T(8,128)}, f32[2,256,512]{2,1,0:T(8,128)}, u32[]{:S(2)}, u32[]{:S(2)}) collective-permute-start(f32[2,256,512]{2,1,0:T(8,128)} %collective-permute-done.3.t20), channel_id=1, source_target_pairs={{0,3},{1,0},{2,1},{3,2},{4,7},{5,4},{6,5},{7,6},{8,11},{9,8},{10,9... | collective-permute-start | bytes 3145736 | tf_op jit(solution)/shard_map/ppermute | solution.py:19
  141.1 14.4 %copy-start = (bf16[8,4,4,16,512]{4,3,2,1,0:T(8,128)(2,1)}, bf16[8,4,4,16,512]{4,3,2,1,0:T(8,128)(2,1)S(1)}, u32[]{:S(2)}) copy-start(bf16[8,4,4,16,512]{4,3,2,1,0:T(8,128)(2,1)S(1)} %all-to-all-done.amp) | copy-start | bytes 6291460
  141.1 48.6 %all-to-all-start.2 = ((f32[1,32,16,512]{3,2,0,1:T(8,128)}), f32[1,32,16,512]{3,2,0,1:T(8,128)S(1)}, u32[]{:S(2)}, u32[]{:S(2)}) async-start(f32[1,32,16,512]{3,2,0,1:T(8,128)} %bitcast.8), calls=%async_computation.2 | async-start | bytes 2097152 | tf_op jit(solution)/shard_map/all_to_all | solution.py:255
  189.7 54.4 %all-to-all-start.1 = ((f32[2,32,16,512]{3,2,0,1:T(8,128)}), f32[2,32,16,512]{3,2,0,1:T(8,128)S(1)}, u32[]{:S(2)}, u32[]{:S(2)}) async-start(f32[2,32,16,512]{3,2,0,1:T(8,128)} %copy.11), calls=%async_computation.1 | async-start | bytes 4194304 | tf_op jit(solution)/shard_map/all_to_all | solution.py:255
  195.4 132.3 %all-gather.2.cloned.1.call-start = ((), (), s32[]{:S(2)}) async-start(), calls=%async_computation.3 | async-start | bytes 2162688 | tf_op jit(solution)/shard_map/all_gather | solution.py:290
  195.4 59.1 %collective-permute-start.5 = (f32[2,768,512]{2,1,0:T(8,128)}, f32[2,768,512]{2,1,0:T(8,128)}, u32[]{:S(2)}, u32[]{:S(2)}) collective-permute-start(f32[2,768,512]{2,1,0:T(8,128)} %get-tuple-element.13), channel_id=1, source_target_pairs={{0,1},{1,2},{2,3},{3,0},{4,5},{5,6},{6,7},{7,4},{8,9},{9,10},{10,1... | collective-permute-start | bytes 9437192 | tf_op jit(solution)/shard_map/ppermute | solution.py:19
  195.8 58.7 %copy-start.2 = (f32[2,256,512]{2,1,0:T(8,128)S(1)}, f32[2,256,512]{2,1,0:T(8,128)}, u32[]{:S(2)}) copy-start(f32[2,256,512]{2,1,0:T(8,128)} %get-tuple-element.14) | copy-start | bytes 3145732
  254.5 34.6 %copy-start.1 = (f32[2,256,512]{2,1,0:T(8,128)S(1)}, f32[2,256,512]{2,1,0:T(8,128)}, u32[]{:S(2)}) copy-start(f32[2,256,512]{2,1,0:T(8,128)} %get-tuple-element.12) | copy-start | bytes 3145732
  257.0 32.2 %collective-permute-start.6 = (f32[2,256,512]{2,1,0:T(8,128)S(1)}, f32[2,256,512]{2,1,0:T(8,128)S(1)}, u32[]{:S(2)}, u32[]{:S(2)}) collective-permute-start(f32[2,256,512]{2,1,0:T(8,128)S(1)} %get-tuple-element.18), channel_id=1, source_target_pairs={{0,4},{4,8},{8,12},{12,16},{16,20},{20,24},{24,28},{28,0},{1,5},{5... | collective-permute-start | bytes 3145736 | tf_op jit(solution)/shard_map/ppermute | solution.py:19
  258.5 30.6 %collective-permute-start.7 = (f32[2,256,512]{2,1,0:T(8,128)S(1)}, f32[2,256,512]{2,1,0:T(8,128)S(1)}, u32[]{:S(2)}, u32[]{:S(2)}) collective-permute-start(f32[2,256,512]{2,1,0:T(8,128)S(1)} %get-tuple-element.19), channel_id=1, source_target_pairs={{0,8},{4,12},{8,16},{12,20},{16,24},{20,28},{24,0},{28,4},{1,9},{5... | collective-permute-start | bytes 3145736 | tf_op jit(solution)/shard_map/ppermute | solution.py:19
Sparse Core Ops, SparseCore 0:
  245.1 82.5 all-gather.1

commit v2 on v1

--- a/solution.py
+++ b/solution.py
@@ -1,8 +1,9 @@
-import functools
 import math
 
 import jax
 import jax.numpy as jnp
+import ml_dtypes
+import numpy as np
 from jax import lax
 from jax.experimental import pallas as pl
 from jax.experimental.pallas import tpu as pltpu
@@ -20,13 +21,59 @@
 
 
 def dft_tables(size):
-    index = jnp.arange(size, dtype=jnp.int32)
+    index = np.arange(size, dtype=np.int32)
     wrapped = index[:, None] * index[None, :] % size
-    angle = wrapped.astype(jnp.float32) * (2.0 * math.pi / size)
-    norm = 1.0 / math.sqrt(size)
+    angle = wrapped.astype(np.float32) * np.float32(2.0 * math.pi / size)
+    norm = np.float32(1.0 / math.sqrt(size))
     return (
-        (jnp.cos(angle) * norm).astype(jnp.bfloat16),
-        (-jnp.sin(angle) * norm).astype(jnp.bfloat16),
+        (np.cos(angle) * norm).astype(ml_dtypes.bfloat16),
+        (-np.sin(angle) * norm).astype(ml_dtypes.bfloat16),
+    )
+
+
+def pull_lanes(block, off):
+    turn = lax.rem(LANES - off, LANES)
+    lane = lax.broadcasted_iota(jnp.int32, (block.shape[0], LANES), 1)
+    keep = lane < LANES - off
+    count = block.shape[1] // LANES
+    turned = [pltpu.roll(block[:, i * LANES : (i + 1) * LANES], turn, 1) for i in range(count)]
+    return jnp.concatenate(
+        [jnp.where(keep, turned[i], turned[i + 1]) for i in range(count - 1)], axis=1
+    )
+
+
+def push_lanes(block, off):
+    lane = lax.broadcasted_iota(jnp.int32, (block.shape[0], LANES), 1)
+    keep = lane >= off
+    count = block.shape[1] // LANES
+    blank = jnp.zeros((block.shape[0], LANES), block.dtype)
+    turned = [pltpu.roll(block[:, i * LANES : (i + 1) * LANES], off, 1) for i in range(count)]
+    turned = [blank] + turned + [blank]
+    return jnp.concatenate(
+        [jnp.where(keep, turned[i + 1], turned[i]) for i in range(count + 1)], axis=1
+    )
+
+
+def pull_rows(block, off):
+    turn = lax.rem(SUBLANES - off, SUBLANES)
+    row = lax.broadcasted_iota(jnp.int32, (SUBLANES, block.shape[1]), 0)
+    keep = row < SUBLANES - off
+    count = block.shape[0] // SUBLANES
+    turned = [pltpu.roll(block[i * SUBLANES : (i + 1) * SUBLANES], turn, 0) for i in range(count)]
+    return jnp.concatenate(
+        [jnp.where(keep, turned[i], turned[i + 1]) for i in range(count - 1)], axis=0
+    )
+
+
+def push_rows(block, off):
+    row = lax.broadcasted_iota(jnp.int32, (SUBLANES, block.shape[1]), 0)
+    keep = row >= off
+    count = block.shape[0] // SUBLANES
+    blank = jnp.zeros((SUBLANES, block.shape[1]), block.dtype)
+    turned = [pltpu.roll(block[i * SUBLANES : (i + 1) * SUBLANES], off, 0) for i in range(count)]
+    turned = [blank] + turned + [blank]
+    return jnp.concatenate(
+        [jnp.where(keep, turned[i + 1], turned[i]) for i in range(count + 1)], axis=0
     )
 
 
@@ -35,7 +82,8 @@
 
 
 def forward_kernel(
-    offsets, t00, t01, t10, t11, t20, t21, ill, left, right, far, patch, density, region, wave, half, sems
+    offsets, t00, t01, t10, t10_odd, t11, t20, t21, ill, left, right, far, patch, density_out,
+    region, wave, half, density, sems,
 ):
     slot = pl.program_id(0)
     size = ill.shape[-1]
@@ -45,15 +93,27 @@
 
     @pl.when(slot == 0)
     def _():
-        copies = []
-        for at, tile in enumerate((t00, t01, t10, t11, t20, t21)):
+        def move(tile, at):
             down, across = divmod(at, 2)
             place = region.at[:, pl.ds(down * rows, rows), pl.ds(across * cols, cols)]
-            copies.append(pltpu.make_async_copy(tile, place, sems.at[at]))
+            return pltpu.make_async_copy(tile, place, sems.at[at])
+
+        odd = lax.rem(lax.axis_index("row"), 2) == 1
+
+        @pl.when(odd)
+        def _():
+            move(t10_odd, 2).start()
+
+        @pl.when(jnp.logical_not(odd))
+        def _():
+            move(t10, 2).start()
+
+        copies = [move(t00, 0), move(t01, 1), move(t11, 3), move(t20, 4), move(t21, 5)]
         for copy in copies:
             copy.start()
         for copy in copies:
             copy.wait()
+        move(t10, 2).wait()
         density[...] = jnp.zeros_like(density)
 
     row_at = offsets[slot, 0]
@@ -61,8 +121,7 @@
     coarse = row_at - fine
     tall = step + SUBLANES
     base = pl.multiple_of(slot * (cols // pl.num_programs(0)), LANES)
-    shift = lax.rem(wide - (offsets[slot, 1] - base), wide)
-    raised = lax.rem(tall - fine, tall)
+    shift = offsets[slot, 1] - base
 
     def gather(i, carry):
         at = pl.multiple_of(i * step, step)
@@ -71,8 +130,7 @@
         for part in range(2):
             top = pl.multiple_of(coarse + at, SUBLANES)
             block = region[part, pl.ds(top, tall), pl.ds(base, wide)]
-            moved = pltpu.roll(block, shift, 1)[:, :size]
-            parts.append(pltpu.roll(moved, raised, 0)[:step])
+            parts.append(pull_rows(pull_lanes(block, shift), fine))
         real, imag = parts
         patch[0, 0, here, :] = real
         patch[0, 1, here, :] = imag
@@ -89,10 +147,16 @@
     half[:, size:] = mdot(left[size:, :], wave[...]).astype(jnp.bfloat16)
     far[0] = mdot(half[...], right[...])
 
+    @pl.when(slot == pl.num_programs(0) - 1)
+    def _():
+        total = density[...].astype(jnp.bfloat16)
+        density_out[0] = total
+        density_out[1] = total
+
 
 def backward_kernel(
-    offsets, module_row, amp, far, patch, ill, left, right, upper, middle, lower, side, numer,
-    frame, accum, corr, back, change,
+    offsets, module_row, amp, far, patch, ill, left, right, upper, middle, lower, side, numer_out,
+    frame, accum, corr, back, change, numer,
 ):
     slot = pl.program_id(0)
     size = ill.shape[-1]
@@ -116,8 +180,9 @@
         here = pl.ds(at, step)
         real = far[0, here, :size]
         imag = far[0, here, size:]
-        magnitude = jnp.sqrt(real * real + imag * imag)
-        factor = frame[here, :].astype(jnp.float32) / jnp.maximum(magnitude, 0.25) - 1.0
+        power = real * real + imag * imag
+        inverse = lax.rsqrt(jnp.maximum(power, 0.0625))
+        factor = frame[here, :].astype(jnp.float32) * inverse - 1.0
         corr[here, :] = (factor * real).astype(jnp.bfloat16)
         low = pl.ds(pl.multiple_of(size + at, step), step)
         corr[low, :] = (factor * imag).astype(jnp.bfloat16)
@@ -134,8 +199,6 @@
     tall = step + SUBLANES
     base = pl.multiple_of(slot * (cols // pl.num_programs(0)), LANES)
     shift = offsets[slot, 1] - base
-    blank_below = jnp.zeros((SUBLANES, size), jnp.float32)
-    blank_beside = jnp.zeros((tall, LANES), jnp.float32)
 
     def spread(i, carry):
         at = pl.multiple_of(i * step, step)
@@ -153,8 +216,7 @@
             ill_real * chg_imag - ill_imag * chg_real,
         )
         for part in range(2):
-            moved = pltpu.roll(jnp.concatenate([grads[part], blank_below], axis=0), fine, 0)
-            moved = pltpu.roll(jnp.concatenate([moved, blank_beside], axis=1), shift, 1)
+            moved = push_lanes(push_rows(grads[part], fine), shift)
             top = pl.multiple_of(coarse + at, SUBLANES)
             accum[part, pl.ds(top, tall), pl.ds(base, wide)] += moved
         return carry
@@ -167,6 +229,7 @@
         middle[...] = accum[:, rows : 2 * rows, :cols]
         lower[...] = accum[:, 2 * rows :, :cols]
         side[...] = accum[:, :, cols:]
+        numer_out[...] = numer[...].astype(jnp.bfloat16)
 
 
 def whole():
@@ -181,22 +244,23 @@
         forward_kernel,
         grid=(slots,),
         in_specs=[pl.BlockSpec(memory_space=pltpu.SMEM)]
-        + [pl.BlockSpec(memory_space=pl.ANY)] * 6
+        + [pl.BlockSpec(memory_space=pl.ANY)] * 7
         + [whole()] * 3,
         out_specs=[
             pl.BlockSpec((1, size, 2 * size), lambda s: (s, 0, 0)),
             pl.BlockSpec((1, 2, size, size), lambda s: (s, 0, 0, 0)),
-            pl.BlockSpec((size, size), lambda s: (0, 0)),
+            pl.BlockSpec((2, size, size), lambda s: (0, 0, 0)),
         ],
         out_shape=[
             jax.ShapeDtypeStruct((slots, size, 2 * size), jnp.float32),
             jax.ShapeDtypeStruct((slots, 2, size, size), jnp.float32),
-            jax.ShapeDtypeStruct((size, size), jnp.float32),
+            jax.ShapeDtypeStruct((2, size, size), jnp.bfloat16),
         ],
         scratch_shapes=[
             pltpu.VMEM((2, 3 * rows, 2 * cols), jnp.float32),
             pltpu.VMEM((2 * size, size), jnp.bfloat16),
             pltpu.VMEM((size, 2 * size), jnp.bfloat16),
+            pltpu.VMEM((size, size), jnp.float32),
             pltpu.SemaphoreType.DMA((6,)),
         ],
         compiler_params=pltpu.CompilerParams(vmem_limit_bytes=VMEM_LIMIT),
@@ -232,7 +296,7 @@
             tile,
             tile,
             jax.ShapeDtypeStruct((2, 3 * rows, cols), jnp.float32),
-            jax.ShapeDtypeStruct((2, size, size), jnp.float32),
+            jax.ShapeDtypeStruct((2, size, size), jnp.bfloat16),
         ],
         scratch_shapes=[
             pltpu.VMEM((size, size), jnp.bfloat16),
@@ -240,6 +304,7 @@
             pltpu.VMEM((2 * size, size), jnp.bfloat16),
             pltpu.VMEM((size, 2 * size), jnp.bfloat16),
             pltpu.VMEM((size, 2 * size), jnp.float32),
+            pltpu.VMEM((2, size, size), jnp.float32),
         ],
         compiler_params=pltpu.CompilerParams(vmem_limit_bytes=VMEM_LIMIT),
         cost_estimate=pl.CostEstimate(
@@ -249,11 +314,9 @@
     )(offsets, module_row, amp, far, patch, ill, left, right)
 
 
-def shard_sum(value, devices):
-    parts, size, width = value.shape
-    cut = value.reshape(parts, devices, size // devices, width)
-    got = lax.all_to_all(cut, ("row", "col"), split_axis=1, concat_axis=1, tiled=True)
-    return jnp.sum(got, axis=1)
+def shard_sum(chunks):
+    got = lax.all_to_all(chunks, ("row", "col"), split_axis=0, concat_axis=0, tiled=True)
+    return jnp.sum(got.astype(jnp.float32), axis=0)
 
 
 def shards(measured, module_row, scan_offsets, specimen, illumination):
@@ -262,33 +325,38 @@
     rows, cols = specimen.shape[1:]
     n_row = lax.axis_size("row")
     devices = n_row * lax.axis_size("col")
+    share_rows = 2 * size // devices
     offsets = scan_offsets.reshape(slots, 2)
-    below = passed_along(specimen, "row", -1)
+    odd = lax.rem(lax.axis_index("row"), 2) == 1
     farther = passed_along(specimen, "row", -2)
+    direct = lax.ppermute(specimen, "row", [(at + 1, at) for at in range(0, n_row, 2)])
     beside = passed_along(specimen, "col", -1)
-    below_beside = passed_along(below, "col", -1)
+    cut = measured.reshape((n_row, slots) + measured.shape[1:])
+    cut, farther, direct, beside = lax.optimization_barrier((cut, farther, direct, beside))
+    relayed = lax.ppermute(farther, "row", [(at, at + 1) for at in range(0, n_row, 2)])
     farther_beside = passed_along(farther, "col", -1)
-    cut = measured.reshape((n_row, slots) + measured.shape[1:])
     amp = lax.all_to_all(cut, "row", split_axis=0, concat_axis=0, tiled=True)
+    below_beside = passed_along(jnp.where(odd, relayed, direct), "col", -1)
     cos_table, sin_table = dft_tables(size)
-    left = jnp.block([[cos_table, -sin_table], [sin_table, cos_table]])
-    right = jnp.block([[cos_table, sin_table], [-sin_table, cos_table]])
-    tiles = (specimen, beside, below, below_beside, farther, farther_beside)
+    left = jnp.asarray(np.block([[cos_table, -sin_table], [sin_table, cos_table]]))
+    right = jnp.asarray(np.block([[cos_table, sin_table], [-sin_table, cos_table]]))
+    tiles = (specimen, beside, direct, relayed, below_beside, farther, farther_beside)
     far, patch, density = forward(offsets, tiles, illumination, left, right)
-    density_share = shard_sum(density[None], devices)
+    density_share = shard_sum(density.reshape(devices, share_rows, size))
     upper, middle, lower, side, numer = backward(
         offsets, module_row, amp, far, patch, illumination, left, right, rows, cols
     )
+    numer_share = shard_sum(numer.reshape(devices, share_rows, size))
     got = passed_along(side, "col", 1)
-    middle = middle + got[:, rows : 2 * rows]
-    lower = lower + got[:, 2 * rows :]
-    specimen_step = (
-        upper + got[:, :rows] + passed_along(middle, "row", 1) + passed_along(lower, "row", 2)
-    )
-    numer_share = shard_sum(numer, devices)
     share = numer_share / jnp.sqrt(density_share + 1e-06)
-    illumination_step = lax.all_gather(share, ("row", "col"), axis=1, tiled=True)
-    return (specimen_step, illumination_step)
+    got, _ = lax.optimization_barrier((got, share))
+    gathered = lax.all_gather(share, ("row", "col"), axis=0, tiled=True)
+    middle = (middle + got[:, rows : 2 * rows]).astype(jnp.bfloat16)
+    lower = (lower + got[:, 2 * rows :]).astype(jnp.bfloat16)
+    middle = passed_along(middle, "row", 1).astype(jnp.float32)
+    lower = passed_along(lower, "row", 2).astype(jnp.float32)
+    specimen_step = upper + got[:, :rows] + middle + lower
+    return (specimen_step, gathered.reshape(2, size, size))
 
 
 def solution(mesh):

time: 338 us -> 277 us (0.82)
  waiting for transfers between devices: 199 us -> 162 us
  other arithmetic: 24.4 us -> 6.7 us
  Pallas kernels: 57.3 us -> 51.4 us
    ppermute x8 -> x7, waiting for transfers between devices: 115 us -> 51.5 us  [passed_along(): return lax.ppermute(value, axis, pairs)]
    ppermute x0 -> x2, waiting for transfers between devices: none -> 59.5 us  [the longest x1 39 us: shards(): lax.ppermute(farther, 'row', [(at, at + 1) for at in range(0, n_row, 2)])]
    all_to_all x2, waiting for transfers between devices: 48.3 us -> 25.7 us  [shard_sum(): lax.all_to_all(chunks, ('row', 'col'), split_axis=0, concat_axis=0, tiled...]
    all_gather x1, waiting for transfers between devices: 35.9 us -> 24.8 us  [shards(): gathered = lax.all_gather(share, ('row', 'col'), axis=0, tiled=True)]
    concatenate x1 -> x0, other arithmetic: 10 us -> none  [shards(): right = jnp.block([[cos_table, sin_table], [-sin_table, cos_table]])]
    ppermute x0 -> x2, starting transfers between devices: none -> 6.34 us  [the longest x1 5.04 us: shards(): lax.ppermute(farther, 'row', [(at, at + 1) for at in range(0, n_row, 2)])]
    all_to_all x2, starting transfers between devices: 20 us -> 15 us  [shard_sum(): lax.all_to_all(chunks, ('row', 'col'), split_axis=0, concat_axis=0, tiled...]
    neg x1 -> x0, other arithmetic: 3.99 us -> none  [shards(): left = jnp.block([[cos_table, -sin_table], [sin_table, cos_table]])]
  transfers between devices with their start and end apart: 12 -> 13, of which waited for: 6 -> 8; matrix products, arithmetic and copies ran while one was open for 8% -> 3% of each run, Pallas kernels for 17% -> 19%
where the time goes in v2:
time: 277 us; the launch traced here: 276 us
  waiting for transfers between devices  162 us (58%)
  Pallas kernels  51.4 us (19%)
  starting transfers between devices  37.8 us (14%)
  between operations  14.1 us (5%)
  other arithmetic  6.7 us (2%)
  local copies, waits for them, and re-layouts  4.74 us (2%)
    ppermute x7, waiting for transfers between devices, passed_along(): return lax.ppermute(value, axis, pairs)  51.5 us
    ppermute x1, waiting for transfers between devices, shards(): lax.ppermute(farther, 'row', [(at, at + 1) for at in range(0, n_row, 2)])  39 us
    pallas_call x1, Pallas kernels, backward(): pl.pallas_call(backward_kernel, grid=(slots,), in_specs=[scalar, scalar,...  27.1 us
    all_to_all x2, waiting for transfers between devices, shard_sum(): lax.all_to_all(chunks, ('row', 'col'), split_axis=0, concat_axis=0, tiled...  25.7 us
    all_gather x1, waiting for transfers between devices, shards(): gathered = lax.all_gather(share, ('row', 'col'), axis=0, tiled=True)  24.8 us
    pallas_call x1, Pallas kernels, forward(): pl.pallas_call(forward_kernel, grid=(slots,), in_specs=[pl.BlockSpec(memo...  24.3 us
    ppermute x1, waiting for transfers between devices, shards(): lax.ppermute(specimen, 'row', [(at + 1, at) for at in range(0, n_row, 2)])  20.5 us
    all_to_all x2, starting transfers between devices, shard_sum(): lax.all_to_all(chunks, ('row', 'col'), split_axis=0, concat_axis=0, tiled...  15 us
  transfers between devices with their start and end apart: 13, of which 8 were waited for; matrix products, arithmetic and copies ran while one was open for 3% of the time, Pallas kernels for 19%

profile of v2, /device:TPU:0, one launch (start us, length us, event | category | flops | bytes accessed | tf_op | source)
XLA Modules:
  0.0 276.4 jit_solution(6421784673440992002)
XLA Ops:
  7.2 1.3 collective-permute-start.1
  8.5 5.1 %collective-permute-start = (f32[2,256,512]{2,1,0:T(8,128)}, f32[2,256,512]{2,1,0:T(8,128)}, u32[]{:S(2)}, u32[]{:S(2)}) collective-permute-start(f32[2,256,512]{2,1,0:T(8,128)} %t00.1), channel_id=1, source_target_pairs={{0,24},{4,28},{8,0},{12,4},{16,8},{20,12},{24,16},{28,20},{1,25},{... | collective-permute-start | bytes 3145736 | tf_op jit(solution)/shard_map/ppermute | solution.py:20
  13.6 0.7 collective-permute-start.2
  14.2 20.5 %collective-permute-done.1.t10 = f32[2,256,512]{2,1,0:T(8,128)S(1)} collective-permute-done((f32[2,256,512]{2,1,0:T(8,128)}, f32[2,256,512]{2,1,0:T(8,128)S(1)}, u32[]{:S(2)}, u32[]{:S(2)}) %collective-permute-start.1) | collective-permute-done | bytes 1048608 | tf_op jit(solution)/shard_map/ppermute | solution.py:332
  34.8 1.5 collective-permute-done.t20
  36.3 7.4 %all-to-all-start = ((bf16[8,4,4,16,512]{4,3,2,1,0:T(8,128)(2,1)}), bf16[8,4,4,16,512]{4,3,2,1,0:T(8,128)(2,1)S(1)}, u32[]{:S(2)}, u32[]{:S(2)}) async-start(bf16[8,4,4,16,512]{4,3,2,1,0:T(8,128)(2,1)} %bitcast.5), calls=%async_computation | async-start | bytes 4194304 | tf_op jit(solution)/shard_map/all_to_all | solution.py:338
  43.7 5.0 %collective-permute-start.3 = (f32[2,256,512]{2,1,0:T(8,128)}, f32[2,256,512]{2,1,0:T(8,128)}, u32[]{:S(2)}, u32[]{:S(2)}) collective-permute-start(f32[2,256,512]{2,1,0:T(8,128)} %collective-permute-done.t20), channel_id=1, source_target_pairs={{0,4},{8,12},{16,20},{24,28},{1,5},{9,13},{17,21},{25,29},{2,6},{1... | collective-permute-start | bytes 3145736 | tf_op jit(solution)/shard_map/ppermute | solution.py:336
  48.8 39.0 %collective-permute-done.3.t10_odd = f32[2,256,512]{2,1,0:T(8,128)} collective-permute-done((f32[2,256,512]{2,1,0:T(8,128)}, f32[2,256,512]{2,1,0:T(8,128)}, u32[]{:S(2)}, u32[]{:S(2)}) %collective-permute-start.3) | collective-permute-done | bytes 1048608 | tf_op jit(solution)/shard_map/ppermute | solution.py:336
  87.7 1.2 broadcast_select_fusion
  88.9 0.7 copy.10.offsets
  89.6 12.0 %collective-permute-done.4.t11 = f32[2,256,512]{2,1,0:T(8,128)S(1)} collective-permute-done((f32[2,256,512]{2,1,0:T(8,128)}, f32[2,256,512]{2,1,0:T(8,128)S(1)}, u32[]{:S(2)}, u32[]{:S(2)}) %collective-permute-start.4) | collective-permute-done | bytes 1048608 | tf_op jit(solution)/shard_map/ppermute | solution.py:20
  101.6 1.0 copy-done.6
  102.5 24.3 %forward.1 = (f32[4,512,1024]{2,1,0:T(8,128)}, f32[4,2,512,512]{3,2,1,0:T(8,128)}, bf16[2,512,512]{2,1,0:T(8,128)(2,1)}) custom-call(s32[4,2]{1,0:T(4,128)} %copy.10.offsets, f32[2,256,512]{2,1,0:T(8,128)} %t00.1, f32[2,256,512]{2,1,0:T(8,128)} %collective-permute-done.2.t01, f32[2,256,512]{2,1,0:T(8,128)} %copy-done.3, ...), custom_call_target="tpu_custom_call" | custom-call | flops 8589934592 | bytes 29360128 | tf_op jit(solution)/shard_map/forward/pallas_call | solution.py:243
  126.8 0.0 copy-start
  126.8 9.1 %all-to-all-start.2 = ((bf16[32,32,512]{2,1,0:T(8,128)(2,1)}), bf16[32,32,512]{2,1,0:T(8,128)(2,1)S(1)}, u32[]{:S(2)}, u32[]{:S(2)}) async-start(bf16[32,32,512]{2,1,0:T(8,128)(2,1)} %bitcast.8), calls=%async_computation.2 | async-start | bytes 2097152 | tf_op jit(solution)/shard_map/all_to_all | solution.py:318
  136.0 27.1 %backward.1 = (f32[2,256,512]{2,1,0:T(8,128)}, f32[2,256,512]{2,1,0:T(8,128)}, f32[2,256,512]{2,1,0:T(8,128)}, f32[2,768,512]{2,1,0:T(8,128)}, bf16[2,512,512]{2,1,0:T(8,128)(2,1)}) custom-call(s32[4,2]{1,0:T(4,128)} %copy.10.offsets, s32[32]{0:T(128)} %module_row.1, bf16[8,4,4,16,512]{4,3,2,1,0:T(8,128)(2,1)} %copy-done, ...), custom_call_target="tpu_custom_call" | custom-call | flops 8589934592 | bytes 29360128 | tf_op jit(solution)/shard_map/backward/pallas_call | solution.py:280
  163.1 5.8 %all-to-all-start.1 = ((bf16[32,32,512]{2,1,0:T(8,128)(2,1)}), bf16[32,32,512]{2,1,0:T(8,128)(2,1)S(1)}, u32[]{:S(2)}, u32[]{:S(2)}) async-start(bf16[32,32,512]{2,1,0:T(8,128)(2,1)} %bitcast.7), calls=%async_computation.1 | async-start | bytes 2097152 | tf_op jit(solution)/shard_map/all_to_all | solution.py:318
  169.0 0.0 all-gather.2.cloned.1.call-start
  169.0 0.3 collective-permute-start.6
  169.3 0.2 convert_reduce_fusion
  169.5 25.7 %all-to-all-done.1 = bf16[32,32,512]{2,1,0:T(8,128)(2,1)S(1)} async-done(((bf16[32,32,512]{2,1,0:T(8,128)(2,1)}), bf16[32,32,512]{2,1,0:T(8,128)(2,1)S(1)}, u32[]{:S(2)}, u32[]{:S(2)}) %all-to-all-start.1) | async-done | bytes 1048608 | tf_op jit(solution)/shard_map/all_to_all | solution.py:318
  195.2 0.2 convert_reduce_fusion.1
  195.4 0.6 rsqrt_multiply_fusion
  196.0 0.0 all-gather.2.cloned.1.call-update
  196.1 21.3 %collective-permute-done.6 = f32[2,768,512]{2,1,0:T(8,128)} collective-permute-done((f32[2,768,512]{2,1,0:T(8,128)}, f32[2,768,512]{2,1,0:T(8,128)}, u32[]{:S(2)}, u32[]{:S(2)}) %collective-permute-start.6) | collective-permute-done | bytes 3145760 | tf_op jit(solution)/shard_map/ppermute | solution.py:20
  217.4 2.0 add_convert_fusion.1
  219.3 1.5 collective-permute-start.7
  220.9 1.5 collective-permute-start.8
  222.3 16.8 %collective-permute-done.7 = bf16[2,256,512]{2,1,0:T(8,128)(2,1)S(1)} collective-permute-done((bf16[2,256,512]{2,1,0:T(8,128)(2,1)S(1)}, bf16[2,256,512]{2,1,0:T(8,128)(2,1)S(1)}, u32[]{:S(2)}, u32[]{:S(2)}) %collective-permute-start.7) | collective-permute-done | bytes 524320 | tf_op jit(solution)/shard_map/ppermute | solution.py:20
  239.1 2.6 convert_add_fusion
  241.7 24.8 %all-gather.2.cloned.1.call-done = f32[1024,512]{1,0:T(8,128)} async-done(((f32[32,512]{1,0:T(8,128)}), f32[1024,512]{1,0:T(8,128)}) %all-gather.2.cloned.1.call-update) | async-done | bytes 2097168 | tf_op jit(solution)/shard_map/all_gather | solution.py:353
  266.5 3.1 %copy.12 = f32[2,512,512]{2,1,0:T(8,128)} copy(f32[2,512,512]{2,1,0:T(8,128)} %bitcast.6) | data formatting | bytes 4194304
  (19 shorter events, 0.0 us)
Async XLA Ops:
  7.2 27.6 %collective-permute-start.1 = (f32[2,256,512]{2,1,0:T(8,128)}, f32[2,256,512]{2,1,0:T(8,128)S(1)}, u32[]{:S(2)}, u32[]{:S(2)}) collective-permute-start(f32[2,256,512]{2,1,0:T(8,128)} %t00.1), channel_id=1, source_target_pairs={{4,0},{12,8},{20,16},{28,24},{5,1},{13,9},{21,17},{29,25},{6,2},{1... | collective-permute-start | bytes 3145736 | tf_op jit(solution)/shard_map/ppermute | solution.py:332
  8.5 27.8 %collective-permute-start = (f32[2,256,512]{2,1,0:T(8,128)}, f32[2,256,512]{2,1,0:T(8,128)}, u32[]{:S(2)}, u32[]{:S(2)}) collective-permute-start(f32[2,256,512]{2,1,0:T(8,128)} %t00.1), channel_id=1, source_target_pairs={{0,24},{4,28},{8,0},{12,4},{16,8},{20,12},{24,16},{28,20},{1,25},{... | collective-permute-start | bytes 3145736 | tf_op jit(solution)/shard_map/ppermute | solution.py:20
  13.6 22.7 %collective-permute-start.2 = (f32[2,256,512]{2,1,0:T(8,128)}, f32[2,256,512]{2,1,0:T(8,128)}, u32[]{:S(2)}, u32[]{:S(2)}) collective-permute-start(f32[2,256,512]{2,1,0:T(8,128)} %t00.1), channel_id=1, source_target_pairs={{0,3},{1,0},{2,1},{3,2},{4,7},{5,4},{6,5},{7,6},{8,11},{9,8},{10,9... | collective-permute-start | bytes 3145736 | tf_op jit(solution)/shard_map/ppermute | solution.py:20
  34.8 53.0 %copy-start.3 = (f32[2,256,512]{2,1,0:T(8,128)}, f32[2,256,512]{2,1,0:T(8,128)S(1)}, u32[]{:S(2)}) copy-start(f32[2,256,512]{2,1,0:T(8,128)S(1)} %collective-permute-done.1.t10) | copy-start | bytes 3145732
  36.3 90.5 %all-to-all-start = ((bf16[8,4,4,16,512]{4,3,2,1,0:T(8,128)(2,1)}), bf16[8,4,4,16,512]{4,3,2,1,0:T(8,128)(2,1)S(1)}, u32[]{:S(2)}, u32[]{:S(2)}) async-start(bf16[8,4,4,16,512]{4,3,2,1,0:T(8,128)(2,1)} %bitcast.5), calls=%async_computation | async-start | bytes 4194304 | tf_op jit(solution)/shard_map/all_to_all | solution.py:338
  43.7 45.2 %copy-start.5 = (s32[1,1,4,2]{2,3,1,0:T(2,128)S(1)}, s32[1,1,4,2]{2,3,1,0:T(2,128)}, u32[]{:S(2)}) copy-start(s32[1,1,4,2]{2,3,1,0:T(2,128)} %param.9) | copy-start | bytes 100
  43.7 44.0 %collective-permute-start.3 = (f32[2,256,512]{2,1,0:T(8,128)}, f32[2,256,512]{2,1,0:T(8,128)}, u32[]{:S(2)}, u32[]{:S(2)}) collective-permute-start(f32[2,256,512]{2,1,0:T(8,128)} %collective-permute-done.t20), channel_id=1, source_target_pairs={{0,4},{8,12},{16,20},{24,28},{1,5},{9,13},{17,21},{25,29},{2,6},{1... | collective-permute-start | bytes 3145736 | tf_op jit(solution)/shard_map/ppermute | solution.py:336
  48.8 40.8 %collective-permute-start.5 = (f32[2,256,512]{2,1,0:T(8,128)}, f32[2,256,512]{2,1,0:T(8,128)}, u32[]{:S(2)}, u32[]{:S(2)}) collective-permute-start(f32[2,256,512]{2,1,0:T(8,128)} %collective-permute-done.t20), channel_id=1, source_target_pairs={{0,3},{1,0},{2,1},{3,2},{4,7},{5,4},{6,5},{7,6},{8,11},{9,8},{10,9... | collective-permute-start | bytes 3145736 | tf_op jit(solution)/shard_map/ppermute | solution.py:20
  88.9 12.6 %collective-permute-start.4 = (f32[2,256,512]{2,1,0:T(8,128)}, f32[2,256,512]{2,1,0:T(8,128)S(1)}, u32[]{:S(2)}, u32[]{:S(2)}) collective-permute-start(f32[2,256,512]{2,1,0:T(8,128)} %broadcast_select_fusion), channel_id=1, source_target_pairs={{0,3},{1,0},{2,1},{3,2},{4,7},{5,4},{6,5},{7,6},{8,11},{9,8},{10,9... | collective-permute-start | bytes 3145736 | tf_op jit(solution)/shard_map/ppermute | solution.py:20
  101.6 1.0 copy-start.6
  126.8 9.2 %copy-start = (bf16[8,4,4,16,512]{4,3,2,1,0:T(8,128)(2,1)}, bf16[8,4,4,16,512]{4,3,2,1,0:T(8,128)(2,1)S(1)}, u32[]{:S(2)}) copy-start(bf16[8,4,4,16,512]{4,3,2,1,0:T(8,128)(2,1)S(1)} %all-to-all-done.amp) | copy-start | bytes 6291460
  126.8 36.3 %all-to-all-start.2 = ((bf16[32,32,512]{2,1,0:T(8,128)(2,1)}), bf16[32,32,512]{2,1,0:T(8,128)(2,1)S(1)}, u32[]{:S(2)}, u32[]{:S(2)}) async-start(bf16[32,32,512]{2,1,0:T(8,128)(2,1)} %bitcast.8), calls=%async_computation.2 | async-start | bytes 2097152 | tf_op jit(solution)/shard_map/all_to_all | solution.py:318
  163.1 54.2 %copy-start.1 = (f32[2,256,512]{2,1,0:T(8,128)S(1)}, f32[2,256,512]{2,1,0:T(8,128)}, u32[]{:S(2)}) copy-start(f32[2,256,512]{2,1,0:T(8,128)} %get-tuple-element.26) | copy-start | bytes 3145732
  163.1 32.1 %all-to-all-start.1 = ((bf16[32,32,512]{2,1,0:T(8,128)(2,1)}), bf16[32,32,512]{2,1,0:T(8,128)(2,1)S(1)}, u32[]{:S(2)}, u32[]{:S(2)}) async-start(bf16[32,32,512]{2,1,0:T(8,128)(2,1)} %bitcast.7), calls=%async_computation.1 | async-start | bytes 2097152 | tf_op jit(solution)/shard_map/all_to_all | solution.py:318
  169.0 97.5 %all-gather.2.cloned.1.call-start = ((), (), s32[]{:S(2)}) async-start(), calls=%async_computation.3 | async-start | bytes 2162688 | tf_op jit(solution)/shard_map/all_gather | solution.py:353
  169.0 48.3 %collective-permute-start.6 = (f32[2,768,512]{2,1,0:T(8,128)}, f32[2,768,512]{2,1,0:T(8,128)}, u32[]{:S(2)}, u32[]{:S(2)}) collective-permute-start(f32[2,768,512]{2,1,0:T(8,128)} %get-tuple-element.22), channel_id=1, source_target_pairs={{0,1},{1,2},{2,3},{3,0},{4,5},{5,6},{6,7},{7,4},{8,9},{9,10},{10,1... | collective-permute-start | bytes 9437192 | tf_op jit(solution)/shard_map/ppermute | solution.py:20
  169.5 47.9 %copy-start.2 = (f32[2,256,512]{2,1,0:T(8,128)S(1)}, f32[2,256,512]{2,1,0:T(8,128)}, u32[]{:S(2)}) copy-start(f32[2,256,512]{2,1,0:T(8,128)} %get-tuple-element.27) | copy-start | bytes 3145732
  217.4 21.7 %copy-start.4 = (f32[2,256,512]{2,1,0:T(8,128)S(1)}, f32[2,256,512]{2,1,0:T(8,128)}, u32[]{:S(2)}) copy-start(f32[2,256,512]{2,1,0:T(8,128)} %get-tuple-element.21) | copy-start | bytes 3145732
  219.3 19.7 %collective-permute-start.7 = (bf16[2,256,512]{2,1,0:T(8,128)(2,1)S(1)}, bf16[2,256,512]{2,1,0:T(8,128)(2,1)S(1)}, u32[]{:S(2)}, u32[]{:S(2)}) collective-permute-start(bf16[2,256,512]{2,1,0:T(8,128)(2,1)S(1)} %get-tuple-element.28), channel_id=1, source_target_pairs={{0,4},{4,8},{8,12},{12,16},{16,20},{20,24},{24,28},{28,0},{1,5},{5... | collective-permute-start | bytes 1572872 | tf_op jit(solution)/shard_map/ppermute | solution.py:20
  220.9 18.2 %collective-permute-start.8 = (bf16[2,256,512]{2,1,0:T(8,128)(2,1)S(1)}, bf16[2,256,512]{2,1,0:T(8,128)(2,1)S(1)}, u32[]{:S(2)}, u32[]{:S(2)}) collective-permute-start(bf16[2,256,512]{2,1,0:T(8,128)(2,1)S(1)} %get-tuple-element.29), channel_id=1, source_target_pairs={{0,8},{4,12},{8,16},{12,20},{16,24},{20,28},{24,0},{28,4},{1,9},{5... | collective-permute-start | bytes 1572872 | tf_op jit(solution)/shard_map/ppermute | solution.py:20
Sparse Core Ops, SparseCore 0:
  196.2 70.2 all-gather.1

commit v3 on v2

--- a/solution.py
+++ b/solution.py
@@ -155,7 +155,7 @@
 
 
 def backward_kernel(
-    offsets, module_row, amp, far, patch, ill, left, right, upper, middle, lower, side, numer_out,
+    offsets, module_row, amp, far, patch, ill, left, right, upper, middle, lower, side, side_low, numer_out,
     frame, accum, corr, back, change, numer,
 ):
     slot = pl.program_id(0)
@@ -228,7 +228,8 @@
         upper[...] = accum[:, :rows, :cols]
         middle[...] = accum[:, rows : 2 * rows, :cols]
         lower[...] = accum[:, 2 * rows :, :cols]
-        side[...] = accum[:, :, cols:]
+        side[...] = accum[:, :rows, cols:]
+        side_low[...] = accum[:, rows:, cols:]
         numer_out[...] = numer[...].astype(jnp.bfloat16)
 
 
@@ -290,12 +291,13 @@
             whole(),
             whole(),
         ],
-        out_specs=[whole()] * 5,
+        out_specs=[whole()] * 6,
         out_shape=[
             tile,
             tile,
             tile,
-            jax.ShapeDtypeStruct((2, 3 * rows, cols), jnp.float32),
+            tile,
+            jax.ShapeDtypeStruct((2, 2 * rows, cols), jnp.float32),
             jax.ShapeDtypeStruct((2, size, size), jnp.bfloat16),
         ],
         scratch_shapes=[
@@ -332,9 +334,10 @@
     direct = lax.ppermute(specimen, "row", [(at + 1, at) for at in range(0, n_row, 2)])
     beside = passed_along(specimen, "col", -1)
     cut = measured.reshape((n_row, slots) + measured.shape[1:])
-    cut, farther, direct, beside = lax.optimization_barrier((cut, farther, direct, beside))
+    farther, direct, beside = lax.optimization_barrier((farther, direct, beside))
     relayed = lax.ppermute(farther, "row", [(at, at + 1) for at in range(0, n_row, 2)])
     farther_beside = passed_along(farther, "col", -1)
+    cut, relayed, farther_beside = lax.optimization_barrier((cut, relayed, farther_beside))
     amp = lax.all_to_all(cut, "row", split_axis=0, concat_axis=0, tiled=True)
     below_beside = passed_along(jnp.where(odd, relayed, direct), "col", -1)
     cos_table, sin_table = dft_tables(size)
@@ -343,19 +346,20 @@
     tiles = (specimen, beside, direct, relayed, below_beside, farther, farther_beside)
     far, patch, density = forward(offsets, tiles, illumination, left, right)
     density_share = shard_sum(density.reshape(devices, share_rows, size))
-    upper, middle, lower, side, numer = backward(
+    upper, middle, lower, side, side_low, numer = backward(
         offsets, module_row, amp, far, patch, illumination, left, right, rows, cols
     )
     numer_share = shard_sum(numer.reshape(devices, share_rows, size))
-    got = passed_along(side, "col", 1)
+    got_low = passed_along(side_low, "col", 1)
     share = numer_share / jnp.sqrt(density_share + 1e-06)
-    got, _ = lax.optimization_barrier((got, share))
+    got_low, side, _ = lax.optimization_barrier((got_low, side, share))
     gathered = lax.all_gather(share, ("row", "col"), axis=0, tiled=True)
-    middle = (middle + got[:, rows : 2 * rows]).astype(jnp.bfloat16)
-    lower = (lower + got[:, 2 * rows :]).astype(jnp.bfloat16)
+    middle = (middle + got_low[:, :rows]).astype(jnp.bfloat16)
+    lower = (lower + got_low[:, rows:]).astype(jnp.bfloat16)
     middle = passed_along(middle, "row", 1).astype(jnp.float32)
     lower = passed_along(lower, "row", 2).astype(jnp.float32)
-    specimen_step = upper + got[:, :rows] + middle + lower
+    got = passed_along(side, "col", 1)
+    specimen_step = upper + got + middle + lower
     return (specimen_step, gathered.reshape(2, size, size))
 
 

time: 277 us -> 255 us (0.921)
  waiting for transfers between devices: 162 us -> 147 us
  starting transfers between devices: 37.8 us -> 31.7 us
    ppermute x1, waiting for transfers between devices: 39 us -> 15 us  [shards(): lax.ppermute(farther, 'row', [(at, at + 1) for at in range(0, n_row, 2)])]
    ppermute x7 -> x8, waiting for transfers between devices: 51.5 us -> 61.5 us  [passed_along(): return lax.ppermute(value, axis, pairs)]
    all_gather x1, waiting for transfers between devices: 24.8 us -> 16.5 us  [shards(): gathered = lax.all_gather(share, ('row', 'col'), axis=0, tiled=True)]
    all_to_all x1, waiting for transfers between devices: 0.01 us -> 7.92 us  [shards(): amp = lax.all_to_all(cut, 'row', split_axis=0, concat_axis=0, tiled=True)]
    all_to_all x2, starting transfers between devices: 15 us -> 9.52 us  [shard_sum(): lax.all_to_all(chunks, ('row', 'col'), split_axis=0, concat_axis=0, tiled...]
    ppermute x7 -> x8, starting transfers between devices: 9.07 us -> 8.02 us  [passed_along(): return lax.ppermute(value, axis, pairs)]
  transfers between devices with their start and end apart: 13 -> 14, of which waited for: 8 -> 10; matrix products, arithmetic and copies ran while one was open for 3% -> 2% of each run, Pallas kernels for 19% -> 20%
where the time goes in v3:
time: 255 us; the launch traced here: 254 us
  waiting for transfers between devices  147 us (58%)
  Pallas kernels  51.4 us (20%)
  starting transfers between devices  31.7 us (12%)
  between operations  14.1 us (6%)
  local copies, waits for them, and re-layouts  5.65 us (2%)
  other arithmetic  4.08 us (2%)
    ppermute x8, waiting for transfers between devices, passed_along(): return lax.ppermute(value, axis, pairs)  61.5 us
    pallas_call x1, Pallas kernels, backward(): pl.pallas_call(backward_kernel, grid=(slots,), in_specs=[scalar, scalar,...  27.1 us
    all_to_all x2, waiting for transfers between devices, shard_sum(): lax.all_to_all(chunks, ('row', 'col'), split_axis=0, concat_axis=0, tiled...  26 us
    pallas_call x1, Pallas kernels, forward(): pl.pallas_call(forward_kernel, grid=(slots,), in_specs=[pl.BlockSpec(memo...  24.3 us
    ppermute x1, waiting for transfers between devices, shards(): lax.ppermute(specimen, 'row', [(at + 1, at) for at in range(0, n_row, 2)])  20.5 us
    all_gather x1, waiting for transfers between devices, shards(): gathered = lax.all_gather(share, ('row', 'col'), axis=0, tiled=True)  16.5 us
    ppermute x1, waiting for transfers between devices, shards(): lax.ppermute(farther, 'row', [(at, at + 1) for at in range(0, n_row, 2)])  15 us
    all_to_all x2, starting transfers between devices, shard_sum(): lax.all_to_all(chunks, ('row', 'col'), split_axis=0, concat_axis=0, tiled...  9.52 us
  transfers between devices with their start and end apart: 14, of which 10 were waited for; matrix products, arithmetic and copies ran while one was open for 2% of the time, Pallas kernels for 20%

profile of v3, /device:TPU:0, one launch (start us, length us, event | category | flops | bytes accessed | tf_op | source)
XLA Modules:
  0.0 254.5 jit_solution(14139607196636470917)
XLA Ops:
  7.2 1.3 collective-permute-start.1
  8.5 5.1 %collective-permute-start = (f32[2,256,512]{2,1,0:T(8,128)}, f32[2,256,512]{2,1,0:T(8,128)S(1)}, u32[]{:S(2)}, u32[]{:S(2)}) collective-permute-start(f32[2,256,512]{2,1,0:T(8,128)} %t00.1), channel_id=1, source_target_pairs={{0,24},{4,28},{8,0},{12,4},{16,8},{20,12},{24,16},{28,20},{1,25},{... | collective-permute-start | bytes 3145736 | tf_op jit(solution)/shard_map/ppermute | solution.py:20
  13.6 0.7 collective-permute-start.2
  14.2 20.5 %collective-permute-done.1.t10 = f32[2,256,512]{2,1,0:T(8,128)S(1)} collective-permute-done((f32[2,256,512]{2,1,0:T(8,128)}, f32[2,256,512]{2,1,0:T(8,128)S(1)}, u32[]{:S(2)}, u32[]{:S(2)}) %collective-permute-start.1) | collective-permute-done | bytes 1048608 | tf_op jit(solution)/shard_map/ppermute | solution.py:334
  34.8 1.5 collective-permute-done.t20
  36.4 0.9 copy-done.6
  37.3 5.3 %collective-permute-start.3 = (f32[2,256,512]{2,1,0:T(8,128)S(1)}, f32[2,256,512]{2,1,0:T(8,128)}, u32[]{:S(2)}, u32[]{:S(2)}) collective-permute-start(f32[2,256,512]{2,1,0:T(8,128)S(1)} %collective-permute-done.t20), channel_id=1, source_target_pairs={{0,4},{8,12},{16,20},{24,28},{1,5},{9,13},{17,21},{25,29},{2,6},{1... | collective-permute-start | bytes 3145736 | tf_op jit(solution)/shard_map/ppermute | solution.py:338
  42.6 6.1 %collective-permute-done.4.t21 = f32[2,256,512]{2,1,0:T(8,128)S(1)} collective-permute-done((f32[2,256,512]{2,1,0:T(8,128)S(1)}, f32[2,256,512]{2,1,0:T(8,128)S(1)}, u32[]{:S(2)}, u32[]{:S(2)}) %collective-permute-start.4) | collective-permute-done | bytes 1048608 | tf_op jit(solution)/shard_map/ppermute | solution.py:20
  48.7 15.0 %collective-permute-done.3.t10_odd = f32[2,256,512]{2,1,0:T(8,128)} collective-permute-done((f32[2,256,512]{2,1,0:T(8,128)S(1)}, f32[2,256,512]{2,1,0:T(8,128)}, u32[]{:S(2)}, u32[]{:S(2)}) %collective-permute-start.3) | collective-permute-done | bytes 1048608 | tf_op jit(solution)/shard_map/ppermute | solution.py:338
  63.7 7.5 %all-to-all-start = ((bf16[8,4,4,16,512]{4,3,2,1,0:T(8,128)(2,1)}), bf16[8,4,4,16,512]{4,3,2,1,0:T(8,128)(2,1)S(1)}, u32[]{:S(2)}, u32[]{:S(2)}) async-start(bf16[8,4,4,16,512]{4,3,2,1,0:T(8,128)(2,1)} %bitcast.5), calls=%async_computation | async-start | bytes 4194304 | tf_op jit(solution)/shard_map/all_to_all | solution.py:341
  71.3 1.2 broadcast_select_fusion
  72.5 0.7 copy.10.offsets
  73.1 12.0 %collective-permute-done.5.t11 = f32[2,256,512]{2,1,0:T(8,128)S(1)} collective-permute-done((f32[2,256,512]{2,1,0:T(8,128)}, f32[2,256,512]{2,1,0:T(8,128)S(1)}, u32[]{:S(2)}, u32[]{:S(2)}) %collective-permute-start.5) | collective-permute-done | bytes 1048608 | tf_op jit(solution)/shard_map/ppermute | solution.py:20
  85.1 1.0 copy-done.9
  86.1 24.3 %forward.1 = (f32[4,512,1024]{2,1,0:T(8,128)}, f32[4,2,512,512]{3,2,1,0:T(8,128)}, bf16[2,512,512]{2,1,0:T(8,128)(2,1)}) custom-call(s32[4,2]{1,0:T(4,128)} %copy.10.offsets, f32[2,256,512]{2,1,0:T(8,128)} %t00.1, f32[2,256,512]{2,1,0:T(8,128)} %copy-done.7, f32[2,256,512]{2,1,0:T(8,128)} %copy-done.3, f32[2,256,512]{2,1,0:T(8,128)} %collective-permute-done.3.t10_odd, ...), custom_call_target="tpu_custom_call" | custom-call | flops 8589934592 | bytes 29360128 | tf_op jit(solution)/shard_map/forward/pallas_call | solution.py:244
  110.4 7.9 %all-to-all-done.amp = bf16[8,4,4,16,512]{4,3,2,1,0:T(8,128)(2,1)S(1)} async-done(((bf16[8,4,4,16,512]{4,3,2,1,0:T(8,128)(2,1)}), bf16[8,4,4,16,512]{4,3,2,1,0:T(8,128)(2,1)S(1)}, u32[]{:S(2)}, u32[]{:S(2)}) %all-to-all-start) | async-done | bytes 2097184 | tf_op jit(solution)/shard_map/all_to_all | solution.py:341
  118.3 3.7 %all-to-all-start.2 = ((bf16[32,32,512]{2,1,0:T(8,128)(2,1)}), bf16[32,32,512]{2,1,0:T(8,128)(2,1)S(1)}, u32[]{:S(2)}, u32[]{:S(2)}) async-start(bf16[32,32,512]{2,1,0:T(8,128)(2,1)} %bitcast.7), calls=%async_computation.2 | async-start | bytes 2097152 | tf_op jit(solution)/shard_map/all_to_all | solution.py:320
  122.0 27.1 %backward.1 = (f32[2,256,512]{2,1,0:T(8,128)}, f32[2,256,512]{2,1,0:T(8,128)}, f32[2,256,512]{2,1,0:T(8,128)}, f32[2,256,512]{2,1,0:T(8,128)}, f32[2,512,512]{2,1,0:T(8,128)}, /*index=5*/bf16[2,512,512]{2,1,0:T(8,128)(2,1)}) custom-call(s32[4,2]{1,0:T(4,128)} %copy.10.offsets, s32[32]{0:T(128)} %module_row.1, bf16[8,4,4,16,512]{4,3,2,1,0:T(8,128)(2,1)} %copy-done, ...), custom_call_target="tpu_custom_call" | custom-call | flops 8589934592 | bytes 29360128 | tf_op jit(solution)/shard_map/backward/pallas_call | solution.py:281
  149.2 5.8 %all-to-all-start.1 = ((bf16[32,32,512]{2,1,0:T(8,128)(2,1)}), bf16[32,32,512]{2,1,0:T(8,128)(2,1)S(1)}, u32[]{:S(2)}, u32[]{:S(2)}) async-start(bf16[32,32,512]{2,1,0:T(8,128)(2,1)} %bitcast.8), calls=%async_computation.1 | async-start | bytes 2097152 | tf_op jit(solution)/shard_map/all_to_all | solution.py:320
  155.1 0.2 convert_reduce_fusion
  155.2 26.0 %all-to-all-done.1 = bf16[32,32,512]{2,1,0:T(8,128)(2,1)S(1)} async-done(((bf16[32,32,512]{2,1,0:T(8,128)(2,1)}), bf16[32,32,512]{2,1,0:T(8,128)(2,1)S(1)}, u32[]{:S(2)}, u32[]{:S(2)}) %all-to-all-start.1) | async-done | bytes 1048608 | tf_op jit(solution)/shard_map/all_to_all | solution.py:320
  181.3 0.2 convert_reduce_fusion.1
  181.4 0.6 rsqrt_multiply_fusion
  182.1 26.1 %collective-permute-done.6 = f32[2,512,512]{2,1,0:T(8,128)S(1)} collective-permute-done((f32[2,512,512]{2,1,0:T(8,128)}, f32[2,512,512]{2,1,0:T(8,128)S(1)}, u32[]{:S(2)}, u32[]{:S(2)}) %collective-permute-start.6) | collective-permute-done | bytes 2097184 | tf_op jit(solution)/shard_map/ppermute | solution.py:20
  208.3 0.2 collective-permute-start.7
  208.5 0.6 add_convert_fusion.1
  209.0 1.5 collective-permute-start.8
  210.5 0.4 collective-permute-start.9
  210.9 15.8 %collective-permute-done.8 = bf16[2,256,512]{2,1,0:T(8,128)(2,1)S(1)} collective-permute-done((bf16[2,256,512]{2,1,0:T(8,128)(2,1)S(1)}, bf16[2,256,512]{2,1,0:T(8,128)(2,1)S(1)}, u32[]{:S(2)}, u32[]{:S(2)}) %collective-permute-start.8) | collective-permute-done | bytes 524320 | tf_op jit(solution)/shard_map/ppermute | solution.py:20
  226.7 1.4 convert_add_fusion
  228.1 16.5 %all-gather.2.cloned.1.call-done = f32[1024,512]{1,0:T(8,128)} async-done(((f32[32,512]{1,0:T(8,128)}), f32[1024,512]{1,0:T(8,128)}) %all-gather.2.cloned.1.call-update) | async-done | bytes 2097168 | tf_op jit(solution)/shard_map/all_gather | solution.py:356
  244.6 3.1 %copy.12 = f32[2,512,512]{2,1,0:T(8,128)} copy(f32[2,512,512]{2,1,0:T(8,128)} %bitcast.6) | data formatting | bytes 4194304
  (27 shorter events, 0.3 us)
Async XLA Ops:
  7.2 27.6 %collective-permute-start.1 = (f32[2,256,512]{2,1,0:T(8,128)}, f32[2,256,512]{2,1,0:T(8,128)S(1)}, u32[]{:S(2)}, u32[]{:S(2)}) collective-permute-start(f32[2,256,512]{2,1,0:T(8,128)} %t00.1), channel_id=1, source_target_pairs={{4,0},{12,8},{20,16},{28,24},{5,1},{13,9},{21,17},{29,25},{6,2},{1... | collective-permute-start | bytes 3145736 | tf_op jit(solution)/shard_map/ppermute | solution.py:334
  8.5 27.8 %collective-permute-start = (f32[2,256,512]{2,1,0:T(8,128)}, f32[2,256,512]{2,1,0:T(8,128)S(1)}, u32[]{:S(2)}, u32[]{:S(2)}) collective-permute-start(f32[2,256,512]{2,1,0:T(8,128)} %t00.1), channel_id=1, source_target_pairs={{0,24},{4,28},{8,0},{12,4},{16,8},{20,12},{24,16},{28,20},{1,25},{... | collective-permute-start | bytes 3145736 | tf_op jit(solution)/shard_map/ppermute | solution.py:20
  13.6 22.7 %collective-permute-start.2 = (f32[2,256,512]{2,1,0:T(8,128)}, f32[2,256,512]{2,1,0:T(8,128)S(1)}, u32[]{:S(2)}, u32[]{:S(2)}) collective-permute-start(f32[2,256,512]{2,1,0:T(8,128)} %t00.1), channel_id=1, source_target_pairs={{0,3},{1,0},{2,1},{3,2},{4,7},{5,4},{6,5},{7,6},{8,11},{9,8},{10,9... | collective-permute-start | bytes 3145736 | tf_op jit(solution)/shard_map/ppermute | solution.py:20
  34.8 36.5 %copy-start.3 = (f32[2,256,512]{2,1,0:T(8,128)}, f32[2,256,512]{2,1,0:T(8,128)S(1)}, u32[]{:S(2)}) copy-start(f32[2,256,512]{2,1,0:T(8,128)S(1)} %collective-permute-done.1.t10) | copy-start | bytes 3145732
  36.3 1.0 copy-start.6
  36.3 27.4 %copy-start.7 = (f32[2,256,512]{2,1,0:T(8,128)}, f32[2,256,512]{2,1,0:T(8,128)S(1)}, u32[]{:S(2)}) copy-start(f32[2,256,512]{2,1,0:T(8,128)S(1)} %collective-permute-done.2.t01) | copy-start | bytes 3145732
  36.3 12.4 %collective-permute-start.4 = (f32[2,256,512]{2,1,0:T(8,128)S(1)}, f32[2,256,512]{2,1,0:T(8,128)S(1)}, u32[]{:S(2)}, u32[]{:S(2)}) collective-permute-start(f32[2,256,512]{2,1,0:T(8,128)S(1)} %collective-permute-done.t20), channel_id=1, source_target_pairs={{0,3},{1,0},{2,1},{3,2},{4,7},{5,4},{6,5},{7,6},{8,11},{9,8},{10,9... | collective-permute-start | bytes 3145736 | tf_op jit(solution)/shard_map/ppermute | solution.py:20
  37.3 26.4 %collective-permute-start.3 = (f32[2,256,512]{2,1,0:T(8,128)S(1)}, f32[2,256,512]{2,1,0:T(8,128)}, u32[]{:S(2)}, u32[]{:S(2)}) collective-permute-start(f32[2,256,512]{2,1,0:T(8,128)S(1)} %collective-permute-done.t20), channel_id=1, source_target_pairs={{0,4},{8,12},{16,20},{24,28},{1,5},{9,13},{17,21},{25,29},{2,6},{1... | collective-permute-start | bytes 3145736 | tf_op jit(solution)/shard_map/ppermute | solution.py:338
  48.7 15.0 %copy-start.8 = (f32[2,256,512]{2,1,0:T(8,128)}, f32[2,256,512]{2,1,0:T(8,128)S(1)}, u32[]{:S(2)}) copy-start(f32[2,256,512]{2,1,0:T(8,128)S(1)} %collective-permute-done.4.t21) | copy-start | bytes 3145732
  63.7 54.6 %all-to-all-start = ((bf16[8,4,4,16,512]{4,3,2,1,0:T(8,128)(2,1)}), bf16[8,4,4,16,512]{4,3,2,1,0:T(8,128)(2,1)S(1)}, u32[]{:S(2)}, u32[]{:S(2)}) async-start(bf16[8,4,4,16,512]{4,3,2,1,0:T(8,128)(2,1)} %bitcast.5), calls=%async_computation | async-start | bytes 4194304 | tf_op jit(solution)/shard_map/all_to_all | solution.py:341
  71.2 1.2 copy-start.5
  72.5 12.6 %collective-permute-start.5 = (f32[2,256,512]{2,1,0:T(8,128)}, f32[2,256,512]{2,1,0:T(8,128)S(1)}, u32[]{:S(2)}, u32[]{:S(2)}) collective-permute-start(f32[2,256,512]{2,1,0:T(8,128)} %broadcast_select_fusion), channel_id=1, source_target_pairs={{0,3},{1,0},{2,1},{3,2},{4,7},{5,4},{6,5},{7,6},{8,11},{9,8},{10,9... | collective-permute-start | bytes 3145736 | tf_op jit(solution)/shard_map/ppermute | solution.py:20
  85.1 1.0 copy-start.9
  118.3 3.7 %copy-start = (bf16[8,4,4,16,512]{4,3,2,1,0:T(8,128)(2,1)}, bf16[8,4,4,16,512]{4,3,2,1,0:T(8,128)(2,1)S(1)}, u32[]{:S(2)}) copy-start(bf16[8,4,4,16,512]{4,3,2,1,0:T(8,128)(2,1)S(1)} %all-to-all-done.amp) | copy-start | bytes 6291460
  118.3 30.8 %all-to-all-start.2 = ((bf16[32,32,512]{2,1,0:T(8,128)(2,1)}), bf16[32,32,512]{2,1,0:T(8,128)(2,1)S(1)}, u32[]{:S(2)}, u32[]{:S(2)}) async-start(bf16[32,32,512]{2,1,0:T(8,128)(2,1)} %bitcast.7), calls=%async_computation.2 | async-start | bytes 2097152 | tf_op jit(solution)/shard_map/all_to_all | solution.py:320
  149.2 59.3 %copy-start.1 = (f32[2,256,512]{2,1,0:T(8,128)S(1)}, f32[2,256,512]{2,1,0:T(8,128)}, u32[]{:S(2)}) copy-start(f32[2,256,512]{2,1,0:T(8,128)} %get-tuple-element.33) | copy-start | bytes 3145732
  149.2 32.1 %all-to-all-start.1 = ((bf16[32,32,512]{2,1,0:T(8,128)(2,1)}), bf16[32,32,512]{2,1,0:T(8,128)(2,1)S(1)}, u32[]{:S(2)}, u32[]{:S(2)}) async-start(bf16[32,32,512]{2,1,0:T(8,128)(2,1)} %bitcast.8), calls=%async_computation.1 | async-start | bytes 2097152 | tf_op jit(solution)/shard_map/all_to_all | solution.py:320
  155.0 89.5 %all-gather.2.cloned.1.call-start = ((), (), s32[]{:S(2)}) async-start(), calls=%async_computation.3 | async-start | bytes 2162688 | tf_op jit(solution)/shard_map/all_gather | solution.py:356
  155.2 53.2 %copy-start.2 = (f32[2,256,512]{2,1,0:T(8,128)S(1)}, f32[2,256,512]{2,1,0:T(8,128)}, u32[]{:S(2)}) copy-start(f32[2,256,512]{2,1,0:T(8,128)} %get-tuple-element.35) | copy-start | bytes 3145732
  182.1 26.2 %collective-permute-start.6 = (f32[2,512,512]{2,1,0:T(8,128)}, f32[2,512,512]{2,1,0:T(8,128)S(1)}, u32[]{:S(2)}, u32[]{:S(2)}) collective-permute-start(f32[2,512,512]{2,1,0:T(8,128)} %get-tuple-element.28), channel_id=1, source_target_pairs={{0,1},{1,2},{2,3},{3,0},{4,5},{5,6},{6,7},{7,4},{8,9},{9,10},{10,1... | collective-permute-start | bytes 6291464 | tf_op jit(solution)/shard_map/ppermute | solution.py:20
  208.3 18.5 %collective-permute-start.7 = (f32[2,256,512]{2,1,0:T(8,128)}, f32[2,256,512]{2,1,0:T(8,128)S(1)}, u32[]{:S(2)}, u32[]{:S(2)}) collective-permute-start(f32[2,256,512]{2,1,0:T(8,128)} %get-tuple-element.32), channel_id=1, source_target_pairs={{0,1},{1,2},{2,3},{3,0},{4,5},{5,6},{6,7},{7,4},{8,9},{9,10},{10,1... | collective-permute-start | bytes 3145736 | tf_op jit(solution)/shard_map/ppermute | solution.py:20
  208.4 18.3 %copy-start.4 = (f32[2,256,512]{2,1,0:T(8,128)S(1)}, f32[2,256,512]{2,1,0:T(8,128)}, u32[]{:S(2)}) copy-start(f32[2,256,512]{2,1,0:T(8,128)} %get-tuple-element.27) | copy-start | bytes 3145732
  209.0 17.7 %collective-permute-start.8 = (bf16[2,256,512]{2,1,0:T(8,128)(2,1)S(1)}, bf16[2,256,512]{2,1,0:T(8,128)(2,1)S(1)}, u32[]{:S(2)}, u32[]{:S(2)}) collective-permute-start(bf16[2,256,512]{2,1,0:T(8,128)(2,1)S(1)} %get-tuple-element.36), channel_id=1, source_target_pairs={{0,4},{4,8},{8,12},{12,16},{16,20},{20,24},{24,28},{28,0},{1,5},{5... | collective-permute-start | bytes 1572872 | tf_op jit(solution)/shard_map/ppermute | solution.py:20
  210.5 16.2 %collective-permute-start.9 = (bf16[2,256,512]{2,1,0:T(8,128)(2,1)S(1)}, bf16[2,256,512]{2,1,0:T(8,128)(2,1)S(1)}, u32[]{:S(2)}, u32[]{:S(2)}) collective-permute-start(bf16[2,256,512]{2,1,0:T(8,128)(2,1)S(1)} %get-tuple-element.37), channel_id=1, source_target_pairs={{0,8},{4,12},{8,16},{12,20},{16,24},{20,28},{24,0},{28,4},{1,9},{5... | collective-permute-start | bytes 1572872 | tf_op jit(solution)/shard_map/ppermute | solution.py:20
Sparse Core Ops, SparseCore 0:
  182.2 62.3 all-gather.1
